TPU v7x, 32 devices: a whole 2x2x4 slice. The times are simulated.
32 devices in a mesh: ka: 4 (over z), row: 4 (over y, x), col: 2 (over core).
Axes of the slice: x: 2, y: 2, z: 4, core: 2. Of those that a mesh axis runs over, the one named last changes fastest.
Arguments:
- exciton: bfloat16 [4, 4, 128, 128], P('ka'), may hold values from -6 to 6
- orb_cond: bfloat16 [4, 128, 2048], P('ka', None, 'row'), may hold values from -0.5 to 0.5
- orb_val: bfloat16 [4, 128, 2048], P('ka', None, 'col'), may hold values from -0.5 to 0.5
- screened: bfloat16 [4, 2048, 2048], P(None, 'row', 'col'), may hold values from -3 to 3
- q_table: int32 [4, 4], replicated, may hold values from 0 to 3, as said below
Outputs:
- applied: float32 [4, 4, 128, 128], P('ka', None, 'col')
Inputs may be any that keep to these rules, and one draw needn't show every extreme that they name: q_table is the difference table of the k-points of a cyclic grid of 4 points under a relabeling of points and of differences: every row and every column holds each of 0 to 3 once.
All inputs are finite; a program needn't handle non-finite values.
Results may differ from a plain program's by a relative error of at most 0.019.
Values may be sent and summed in bfloat16 or wider, within the bound.
No kernel may reach another device: no remote copies, remote signals or barrier semaphores. Data moves between devices by JAX's collectives and lax.ppermute only.
A program may use at most 64 MiB of HBM per device.

v0:
```python
import functools
import math

import jax
import jax.numpy as jnp
from jax import lax
from jax.experimental import pallas as pl
from jax.experimental.pallas import tpu as pltpu
from jax.sharding import PartitionSpec as P

BF16 = jnp.bfloat16
F32 = jnp.float32
LANES = 128
ROWS = 16
TILE = 128
CHUNK = 256
QUARTERS = 4
MIB = 2**20
JOIN_FLOPS = 2 * 10**10
SPREAD_FLOPS = 2 * 10**10
PANEL_FLOPS = 10**9
IN_HBM = pl.BlockSpec(memory_space=pltpu.HBM)
IN_VMEM = pl.BlockSpec(memory_space=pltpu.VMEM)
IN_SMEM = pl.BlockSpec(memory_space=pltpu.SMEM)


def swap(value, axis, size, flip):
    return lax.ppermute(value, axis, [(i, i ^ flip) for i in range(size)])


def run(copies):
    for copy in copies:
        copy.start()
    for copy in copies:
        copy.wait()


def pack_kernel(n_col, exciton_ref, cond_ref, after_ref, core_ref, sems):
    del after_ref
    col = lax.axis_index("col")
    copies, at = [], 0
    for source in (cond_ref, exciton_ref):
        part = source.shape[0] // n_col
        rows = pl.ds(pl.multiple_of(col * part, part), part)
        for block in range(source.shape[1] // LANES):
            copies.append(pltpu.make_async_copy(
                source.at[rows, block * LANES:(block + 1) * LANES],
                core_ref.at[at:at + part, :], sems.at[len(copies)],
            ))
            at += part
    run(copies)


def join_kernel(*refs):
    *parts, out = refs
    at = 0
    for part in parts:
        out[at:at + part.shape[0], :] = part[...]
        at += part.shape[0]


def join(parts):
    shape = (sum(part.shape[0] for part in parts), parts[0].shape[1])
    return pl.pallas_call(
        join_kernel,
        in_specs=[IN_VMEM] * len(parts),
        out_specs=IN_VMEM,
        out_shape=jax.ShapeDtypeStruct(shape, BF16),
        compiler_params=pltpu.CompilerParams(vmem_limit_bytes=4 * MIB),
        cost_estimate=pl.CostEstimate(flops=JOIN_FLOPS, bytes_accessed=0, transcendentals=0),
        name="join",
    )(*parts)


def spread_kernel(n_row, *refs):
    *parts, out = refs
    row = lax.axis_index("row")
    part = out.shape[1] // n_row
    for other in range(n_row):
        rows = pl.ds(pl.multiple_of((row ^ other) * part, part), part)
        for flip in range(out.shape[0]):
            out[flip, rows, :] = parts[other][flip * part:(flip + 1) * part, :]


def set_panels(panels, cond_tile, exciton, n_v):
    by_point = lax.dot_general(
        cond_tile, exciton, (((0,), (1,)), ((), ())), preferred_element_type=F32
    ).astype(BF16)
    for b in range(exciton.shape[0] // n_v):
        panels[b * TILE:(b + 1) * TILE, :] = by_point[:, b * n_v:(b + 1) * n_v]


def own_kernel(
    q_ref, w_ref, exciton_ref, cond_ref, val_ref, after_ref, sums, w, cond, val, w_own, exciton, panels, sems
):
    del after_ref
    me, n_others = lax.axis_index("ka"), w.shape[0]
    pairs = [(exciton_ref, exciton), (cond_ref, cond), (val_ref, val)]
    pairs += [(w_ref.at[q_ref[me, me]], w_own)]
    pairs += [(w_ref.at[q_ref[me ^ flip, me]], w.at[flip - 1]) for flip in range(1, n_others + 1)]
    copies = [
        pltpu.make_async_copy(source, target, sems.at[i])
        for i, (source, target) in enumerate(pairs)
    ]
    for copy in copies:
        copy.start()
    for copy in copies[:4]:
        copy.wait()
    n_v, n_nu = val.shape
    n_b = exciton.shape[0] // n_v
    for t in range(cond.shape[1] // TILE):
        set_panels(panels.at[t % 2], cond[:, t * TILE:(t + 1) * TILE], exciton[...], n_v)
        for j in range(n_nu // CHUNK):
            at = slice(j * CHUNK, (j + 1) * CHUNK)
            product = jnp.dot(panels[t % 2], val[:, at], preferred_element_type=F32)
            weights = w_own[t * TILE:(t + 1) * TILE, at].astype(F32)
            for b in range(n_b):
                rows = slice(b * TILE, (b + 1) * TILE)
                sums[t, rows, at] = product[rows, :] * weights
    for copy in copies[4:]:
        copy.wait()


def put_together(cores, col, cond, exciton):
    n_col, n_c, n_mu = len(cores), cond.shape[0], cond.shape[1]
    part_c, part_x = n_c // n_col, exciton.shape[0] // n_col
    for other, source in enumerate(cores):
        at = 0
        rows = pl.ds(pl.multiple_of((col ^ other) * part_c, part_c), part_c)
        for block in range(n_mu // LANES):
            cond[rows, block * LANES:(block + 1) * LANES] = source[at:at + part_c, :]
            at += part_c
        rows = pl.ds(pl.multiple_of((col ^ other) * part_x, part_x), part_x)
        exciton[rows, :] = source[at:at + part_x, :]


def panels_kernel(n_col, n_v, *refs):
    *cores, panels, cond, exciton = refs
    col = lax.axis_index("col")
    for i in range(panels.shape[0]):
        put_together(cores[i * n_col:(i + 1) * n_col], col, cond.at[i], exciton.at[i])
        for t in range(panels.shape[1]):
            set_panels(panels.at[i, t], cond[i, :, t * TILE:(t + 1) * TILE], exciton[i], n_v)


def after_kernel(*refs):
    refs[-1][...] = refs[0][...]


def after(value, *others, flops=0):
    return pl.pallas_call(
        after_kernel,
        in_specs=[IN_VMEM] + [pl.BlockSpec(memory_space=pl.ANY)] * len(others),
        out_specs=IN_VMEM,
        out_shape=jax.ShapeDtypeStruct(value.shape, value.dtype),
        compiler_params=pltpu.CompilerParams(vmem_limit_bytes=4 * MIB),
        cost_estimate=pl.CostEstimate(flops=flops, bytes_accessed=0, transcendentals=0),
        name="after",
    )(value, *others)


def direct_kernel(sizes, early, factor, *refs):
    n_ka, n_row, n_col = sizes
    refs = list(refs)

    def take(count):
        taken, refs[:] = refs[:count], refs[count:]
        return taken

    sums, w, cond_own, val_own, early_panels = take(5)
    n_early = early_panels.shape[0]
    late = [flip for flip in range(1, n_ka) if flip not in early]
    cores = [take(n_col) for _ in late]
    val_ref, = take(1)
    keep, *sent = take(n_col)
    x_all, cond_all, panels, products, direct, running, half, total = refs
    col = lax.axis_index("col")
    n_v, n_nu = val_own.shape
    n_c, n_mu = cond_own.shape
    n_b = x_all.shape[1] // n_v
    n_tiles, n_others = n_mu // TILE, n_ka - 1
    order = list(early) + late

    for i in range(len(late)):
        put_together(cores[i], col, cond_all.at[i], x_all.at[i])

    steps = [(t, j) for t in range(n_tiles) for j in range(n_nu // CHUNK)]
    quarter = TILE // QUARTERS

    def all_panels(t):
        for i in range(len(late)):
            set_panels(panels.at[t % 2, i], cond_all[i, :, t * TILE:(t + 1) * TILE], x_all[i], n_v)

    def multiply(number, i):
        t, j = steps[number]
        left = early_panels[i, t] if i < n_early else panels[t % 2, i - n_early]
        products[number % 2, i] = jnp.dot(
            left, val_ref[order[i] - 1, :, j * CHUNK:(j + 1) * CHUNK],
            preferred_element_type=F32,
        ).astype(BF16)

    def combine(number, part):
        t, j = steps[number]
        at = slice(j * CHUNK, (j + 1) * CHUNK)
        for m in range(part * quarter, (part + 1) * quarter, ROWS):
            weights = [
                w[flip - 1, t * TILE + m:t * TILE + m + ROWS, at].astype(F32) for flip in order
            ]
            for b in range(n_b):
                rows = slice(b * TILE + m, b * TILE + m + ROWS)
                value = sums[t, rows, at]
                for i in range(n_others):
                    value += products[number % 2, i, rows, :].astype(F32) * weights[i]
                direct[t % 2, rows, at] = value.astype(BF16)

    def reduce(number):
        t, j = steps[number]
        at = slice(j * CHUNK, (j + 1) * CHUNK)
        value = lax.dot_general(
            direct[t % 2, :, at], val_own[:, at], (((1,), (1,)), ((), ())),
            preferred_element_type=F32,
        )
        if j:
            value += running[...]
        if j + 1 < n_nu // CHUNK:
            running[...] = value
            return
        value = value.astype(BF16)
        for b in range(n_b):
            half[b, t * TILE:(t + 1) * TILE, :] = value[b * TILE:(b + 1) * TILE, :]

    all_panels(0)
    for i in range(n_others):
        multiply(0, i)
    for number, (t, j) in enumerate(steps):
        more = number + 1 < len(steps)
        if more and steps[number + 1][0] != t:
            all_panels(t + 1)
        for i in range(max(n_others, QUARTERS)):
            if more and i < n_others:
                multiply(number + 1, i)
            if i < QUARTERS:
                combine(number, i)
        reduce(number)

    part = n_v // n_col
    for b in range(n_b):
        total[b * n_v:(b + 1) * n_v, :] = (
            jnp.dot(cond_own[...], half[b], preferred_element_type=F32) * factor
        ).T
        for other in range(n_col):
            rows = pl.ds(pl.multiple_of(b * n_v + (col ^ other) * part, part), part)
            value = total[rows, :]
            if other == 0:
                keep[b] = value
            else:
                sent[other - 1][b] = value.astype(BF16)


def local(sizes, exciton, orb_cond, orb_val, screened, q_table):
    n_ka, n_row, n_col = sizes
    n_b, n_v, n_c = exciton.shape[1:]
    x_rows, cond, val, screened, q_table = (
        pltpu.with_memory_space_constraint(array, pltpu.HBM)
        for array in (exciton.reshape(n_b * n_v, n_c), orb_cond[0], orb_val[0], screened, q_table)
    )
    n_mu, n_nu = cond.shape[1], val.shape[1]
    core_rows = (cond.size + x_rows.size) // n_col // LANES
    part = n_v // n_row
    plane = lax.dynamic_slice_in_dim(orb_val[0], lax.axis_index("row") * part, part, 0)
    planes = [swap(plane, "ka", n_ka, flip) for flip in range(1, n_ka)]
    core = pl.pallas_call(
        functools.partial(pack_kernel, n_col),
        in_specs=[IN_HBM] * 2 + [pl.BlockSpec(memory_space=pl.ANY)],
        out_specs=IN_VMEM,
        out_shape=jax.ShapeDtypeStruct((core_rows, LANES), BF16),
        scratch_shapes=[pltpu.SemaphoreType.DMA(((n_mu + n_c) // LANES,))],
        compiler_params=pltpu.CompilerParams(vmem_limit_bytes=4 * MIB),
        name="pack",
    )(x_rows, cond, planes[0])
    joined = join(planes)
    cores = [core]
    for flip in range(1, n_ka):
        last = flip & -flip
        source = cores[flip - last]
        if flip == last and flip > 1:
            source = after(source, planes[flip - 1])
        cores.append(swap(source, "ka", n_ka, last))
        if flip == 2:
            cores[2] = after(cores[2], joined, cores[1])
    n_tiles = n_mu // TILE
    loaded = pl.pallas_call(
        own_kernel,
        in_specs=[IN_SMEM] + [IN_HBM] * 4 + [pl.BlockSpec(memory_space=pl.ANY)],
        out_specs=[IN_VMEM] * 4,
        out_shape=[
            jax.ShapeDtypeStruct((n_tiles, n_b * TILE, n_nu), F32),
            jax.ShapeDtypeStruct((n_ka - 1, n_mu, n_nu), BF16),
            jax.ShapeDtypeStruct(cond.shape, BF16),
            jax.ShapeDtypeStruct(val.shape, BF16),
        ],
        scratch_shapes=[
            pltpu.VMEM((n_mu, n_nu), BF16),
            pltpu.VMEM(x_rows.shape, BF16),
            pltpu.VMEM((2, n_b * TILE, n_v), BF16),
            pltpu.SemaphoreType.DMA((n_ka + 3,)),
        ],
        compiler_params=pltpu.CompilerParams(vmem_limit_bytes=24 * MIB),
        cost_estimate=pl.CostEstimate(
            flops=0, bytes_accessed=4 * screened.size, transcendentals=0
        ),
        name="own_term",
    )(q_table, screened, x_rows, cond, val, cores[n_ka // 2])
    early = [flip for flip in range(1, n_ka) if flip.bit_count() == 1]
    both = {
        flip: [swap(cores[flip], "col", n_col, d) if d else cores[flip] for d in range(n_col)]
        for flip in range(1, n_ka)
    }
    operands = [pl.pallas_call(
        functools.partial(panels_kernel, n_col, n_v),
        in_specs=[IN_VMEM] * (len(early) * n_col),
        out_specs=IN_VMEM,
        out_shape=jax.ShapeDtypeStruct((len(early), n_tiles, n_b * TILE, n_v), BF16),
        scratch_shapes=[
            pltpu.VMEM((len(early), n_c, n_mu), BF16),
            pltpu.VMEM((len(early), n_b * n_v, n_c), BF16),
        ],
        compiler_params=pltpu.CompilerParams(vmem_limit_bytes=12 * MIB),
        cost_estimate=pl.CostEstimate(flops=PANEL_FLOPS, bytes_accessed=0, transcendentals=0),
        name="panels",
    )(*(part for flip in early for part in both[flip]))]
    operands += [part for flip in both if flip not in early for part in both[flip]]
    parts = [swap(joined, "row", n_row, d) if d else joined for d in range(n_row)]
    operands.append(pl.pallas_call(
        functools.partial(spread_kernel, n_row),
        in_specs=[IN_VMEM] * n_row,
        out_specs=IN_VMEM,
        out_shape=jax.ShapeDtypeStruct((n_ka - 1, *val.shape), BF16),
        compiler_params=pltpu.CompilerParams(vmem_limit_bytes=4 * MIB),
        cost_estimate=pl.CostEstimate(flops=SPREAD_FLOPS, bytes_accessed=0, transcendentals=0),
        name="spread",
    )(*parts))

    factor = math.sqrt(n_v * n_c) / (n_mu * n_row)
    part = n_v // n_col
    n_late = n_ka - 1 - len(early)
    kept, *sent = pl.pallas_call(
        functools.partial(direct_kernel, sizes, early, factor),
        in_specs=[IN_VMEM] * (len(loaded) + len(operands)),
        out_specs=[IN_VMEM] * n_col,
        out_shape=[jax.ShapeDtypeStruct((n_b, part, n_c), F32)]
        + [jax.ShapeDtypeStruct((n_b, part, n_c), BF16)] * (n_col - 1),
        scratch_shapes=[
            pltpu.VMEM((n_late, n_b * n_v, n_c), BF16),
            pltpu.VMEM((n_late, n_c, n_mu), BF16),
            pltpu.VMEM((2, n_late, n_b * TILE, n_v), BF16),
            pltpu.VMEM((2, n_ka - 1, n_b * TILE, CHUNK), BF16),
            pltpu.VMEM((2, n_b * TILE, n_nu), BF16),
            pltpu.VMEM((n_b * TILE, n_v), F32),
            pltpu.VMEM((n_b, n_mu, n_v), BF16),
            pltpu.VMEM((n_b * n_v, n_c), F32),
        ],
        compiler_params=pltpu.CompilerParams(vmem_limit_bytes=36 * MIB),
        name="direct_term",
    )(*loaded, *operands)
    mine = kept
    for flip in range(1, n_col):
        mine = mine + swap(sent[flip - 1], "col", n_col, flip).astype(F32)
    mine = mine.astype(BF16)
    terms = [after(swap(mine, "row", n_row, n_row - 1), flops=JOIN_FLOPS)]
    terms += [swap(mine, "row", n_row, flip) for flip in reversed(range(1, n_row - 1))] + [mine]
    terms = [term.astype(F32) for term in terms]
    while len(terms) > 1:
        terms = [a + b for a, b in zip(terms[::2], terms[1::2])]
    return terms[0][None]


def solution(mesh):
    placed = (
        P("ka", None, None, None),
        P("ka", None, "row"),
        P("ka", None, "col"),
        P(None, "row", "col"),
        P(),
    )
    sizes = tuple(mesh.shape[name] for name in ("ka", "row", "col"))
    return jax.shard_map(
        functools.partial(local, sizes), mesh=mesh, in_specs=placed,
        out_specs=P("ka", None, "col", None), check_vma=False,
    )
```

profile of v0, /device:TPU:0, one launch (start us, length us, event | category | flops | bytes accessed | tf_op | source)
XLA Modules:
  0.0 39.7 jit_solution(9947011263811878443)
XLA Ops:
  0.0 0.8 %dynamic-slice_bitcast_fusion = bf16[32,1024]{1,0:T(8,128)(2,1)S(1)} fusion(bf16[1,128,1024]{2,1,0:T(8,128)(2,1)} %param.7, s32[]{:T(128)S(6)} %select_n.3), kind=kLoop, calls=%fused_computation.2 | loop fusion | bytes 131076 | tf_op jit(solution)/shard_map/dynamic_slice | solution.py:270
  0.8 3.0 %collective-permute-start = (bf16[32,1024]{1,0:T(8,128)(2,1)S(1)}, bf16[32,1024]{1,0:T(8,128)(2,1)S(1)}, u32[]{:S(2)}, u32[]{:S(2)}) collective-permute-start(bf16[32,1024]{1,0:T(8,128)(2,1)S(1)} %dynamic-slice_bitcast_fusion), channel_id=1, source_target_pairs={{0,8},{8,0},{16,24},{24,16},{1,9},{9,1},{17,25},{25,17},{2,10},{10... | collective-permute-start | bytes 196616 | tf_op jit(solution)/shard_map/ppermute | solution.py:28
  3.9 2.6 %collective-permute-start.1 = (bf16[32,1024]{1,0:T(8,128)(2,1)S(1)}, bf16[32,1024]{1,0:T(8,128)(2,1)S(1)}, u32[]{:S(2)}, u32[]{:S(2)}) collective-permute-start(bf16[32,1024]{1,0:T(8,128)(2,1)S(1)} %dynamic-slice_bitcast_fusion), channel_id=1, source_target_pairs={{0,16},{8,24},{16,0},{24,8},{1,17},{9,25},{17,1},{25,9},{2,18},{10... | collective-permute-start | bytes 196616 | tf_op jit(solution)/shard_map/ppermute | solution.py:28
  6.5 0.0 collective-permute-start.3
  6.5 0.0 collective-permute-done.after_ref.refs_0_
  6.5 1.0 %pack.1.refs_0_ = bf16[512,128]{1,0:T(8,128)(2,1)S(1)} custom-call(bf16[512,128]{1,0:T(8,128)(2,1)} %bitcast.7, bf16[128,512]{1,0:T(8,128)(2,1)} %bitcast.9, bf16[32,1024]{1,0:T(8,128)(2,1)S(1)} %collective-permute-done.after_ref.refs_0_), custom_call_target="tpu_custom_call" | custom-call | tf_op jit(solution)/shard_map/pack/pallas_call | solution.py:272
  7.4 1.7 %collective-permute-start.4 = (bf16[512,128]{1,0:T(8,128)(2,1)S(1)}, bf16[512,128]{1,0:T(8,128)(2,1)S(1)}, u32[]{:S(2)}, u32[]{:S(2)}) collective-permute-start(bf16[512,128]{1,0:T(8,128)(2,1)S(1)} %pack.1.refs_0_), channel_id=1, source_target_pairs={{0,8},{8,0},{16,24},{24,16},{1,9},{9,1},{17,25},{25,17},{2,10},{10... | collective-permute-start | bytes 393224 | tf_op jit(solution)/shard_map/ppermute | solution.py:28
  9.2 2.0 %collective-permute-done.1.refs_1_ = bf16[32,1024]{1,0:T(8,128)(2,1)S(1)} collective-permute-done((bf16[32,1024]{1,0:T(8,128)(2,1)S(1)}, bf16[32,1024]{1,0:T(8,128)(2,1)S(1)}, u32[]{:S(2)}, u32[]{:S(2)}) %collective-permute-start.1) | collective-permute-done | bytes 65568 | tf_op jit(solution)/shard_map/ppermute | solution.py:28
  11.2 1.3 %collective-permute-start.2 = (bf16[512,128]{1,0:T(8,128)(2,1)S(1)}, bf16[512,128]{1,0:T(8,128)(2,1)S(1)}, u32[]{:S(2)}, u32[]{:S(2)}) collective-permute-start(bf16[512,128]{1,0:T(8,128)(2,1)S(1)} %after.3), channel_id=1, source_target_pairs={{0,16},{8,24},{16,0},{24,8},{1,17},{9,25},{17,1},{25,9},{2,18},{10... | collective-permute-start | bytes 393224 | tf_op jit(solution)/shard_map/ppermute | solution.py:28
  12.5 0.8 %collective-permute-done.3.refs_2_ = bf16[32,1024]{1,0:T(8,128)(2,1)S(1)} collective-permute-done((bf16[32,1024]{1,0:T(8,128)(2,1)S(1)}, bf16[32,1024]{1,0:T(8,128)(2,1)S(1)}, u32[]{:S(2)}, u32[]{:S(2)}) %collective-permute-start.3) | collective-permute-done | bytes 65568 | tf_op jit(solution)/shard_map/ppermute | solution.py:28
  13.2 2.5 %collective-permute-start.11 = (bf16[96,1024]{1,0:T(8,128)(2,1)S(1)}, bf16[96,1024]{1,0:T(8,128)(2,1)S(1)}, u32[]{:S(2)}, u32[]{:S(2)}) collective-permute-start(bf16[96,1024]{1,0:T(8,128)(2,1)S(1)} %join.1.refs_1_.refs_0_), channel_id=1, source_target_pairs={{0,6},{2,4},{4,2},{6,0},{1,7},{3,5},{5,3},{7,1},{8,14},{10,12},{12... | collective-permute-start | bytes 589832 | tf_op jit(solution)/shard_map/ppermute | solution.py:28
  15.8 0.5 %collective-permute-start.10 = (bf16[96,1024]{1,0:T(8,128)(2,1)S(1)}, bf16[96,1024]{1,0:T(8,128)(2,1)S(1)}, u32[]{:S(2)}, u32[]{:S(2)}) collective-permute-start(bf16[96,1024]{1,0:T(8,128)(2,1)S(1)} %join.1.refs_1_.refs_0_), channel_id=1, source_target_pairs={{0,4},{2,6},{4,0},{6,2},{1,5},{3,7},{5,1},{7,3},{8,12},{10,14},{12... | collective-permute-start | bytes 589832 | tf_op jit(solution)/shard_map/ppermute | solution.py:28
  16.3 0.5 %collective-permute-start.9 = (bf16[96,1024]{1,0:T(8,128)(2,1)S(1)}, bf16[96,1024]{1,0:T(8,128)(2,1)S(1)}, u32[]{:S(2)}, u32[]{:S(2)}) collective-permute-start(bf16[96,1024]{1,0:T(8,128)(2,1)S(1)} %join.1.refs_1_.refs_0_), channel_id=1, source_target_pairs={{0,2},{2,0},{4,6},{6,4},{1,3},{3,1},{5,7},{7,5},{8,10},{10,8},{12,... | collective-permute-start | bytes 589832 | tf_op jit(solution)/shard_map/ppermute | solution.py:28
  16.8 1.9 %collective-permute-done.2.refs_0_ = bf16[512,128]{1,0:T(8,128)(2,1)S(1)} collective-permute-done((bf16[512,128]{1,0:T(8,128)(2,1)S(1)}, bf16[512,128]{1,0:T(8,128)(2,1)S(1)}, u32[]{:S(2)}, u32[]{:S(2)}) %collective-permute-start.2) | collective-permute-done | bytes 131104 | tf_op jit(solution)/shard_map/ppermute | solution.py:28
  18.7 0.0 collective-permute-done.4.refs_2_.refs_0_
  18.7 0.1 collective-permute-start.7
  18.8 0.1 collective-permute-start.6
  18.9 4.1 %own_term.1 = (f32[4,512,1024]{2,1,0:T(8,128)S(1)}, bf16[3,512,1024]{2,1,0:T(8,128)(2,1)S(1)}, bf16[128,512]{1,0:T(8,128)(2,1)S(1)}, bf16[128,1024]{1,0:T(8,128)(2,1)S(1)}) custom-call(s32[4,4]{1,0:T(4,128)} %q_ref.1, bf16[4,512,1024]{2,1,0:T(8,128)(2,1)} %w_ref.1, bf16[512,128]{1,0:T(8,128)(2,1)} %bitcast.8, bf16[128,512]{1,0:T(8,128)(2,1)} %bitcast.10, ...), custom_call_target="tpu_custom_call" | custom-call | bytes 8388608 | tf_op jit(solution)/shard_map/own_term/pallas_call | solution.py:292
  22.9 0.0 collective-permute-done.11.refs_3_
  22.9 0.6 %collective-permute-start.5 = (bf16[512,128]{1,0:T(8,128)(2,1)S(1)}, bf16[512,128]{1,0:T(8,128)(2,1)S(1)}, u32[]{:S(2)}, u32[]{:S(2)}) collective-permute-start(bf16[512,128]{1,0:T(8,128)(2,1)S(1)} %collective-permute-done.4.refs_2_.refs_0_), channel_id=1, source_target_pairs={{0,1},{1,0},{2,3},{3,2},{4,5},{5,4},{6,7},{7,6},{8,9},{9,8},{10,11... | collective-permute-start | bytes 393224 | tf_op jit(solution)/shard_map/ppermute | solution.py:28
  23.5 0.2 collective-permute-done.7.refs_5_
  23.7 0.0 collective-permute-start.8
  23.7 0.0 collective-permute-done.10.refs_2_
  23.7 0.0 collective-permute-done.9.refs_1_
  23.7 0.1 spread.1.refs_7_
  23.8 0.0 collective-permute-done.6.refs_3_
  23.8 0.6 %collective-permute-done.5.refs_1_ = bf16[512,128]{1,0:T(8,128)(2,1)S(1)} collective-permute-done((bf16[512,128]{1,0:T(8,128)(2,1)S(1)}, bf16[512,128]{1,0:T(8,128)(2,1)S(1)}, u32[]{:S(2)}, u32[]{:S(2)}) %collective-permute-start.5) | collective-permute-done | bytes 131104 | tf_op jit(solution)/shard_map/ppermute | solution.py:28
  24.5 0.5 %panels.1.refs_4_ = bf16[2,4,512,128]{3,2,1,0:T(8,128)(2,1)S(1)} custom-call(bf16[512,128]{1,0:T(8,128)(2,1)S(1)} %collective-permute-done.4.refs_2_.refs_0_, bf16[512,128]{1,0:T(8,128)(2,1)S(1)} %collective-permute-done.5.refs_1_, bf16[512,128]{1,0:T(8,128)(2,1)S(1)} %after.4.after_ref.refs_2_, bf16[512,128]{1,0:T(8,128)(2,1)S(1)} %collective-permute-done.6.refs_3_), custom_call_target="tpu_custom_call" | custom-call | flops 1000000000 | tf_op jit(solution)/shard_map/panels/pallas_call | solution.py:319
  25.0 0.1 collective-permute-done.8.refs_6_
  25.1 5.2 %direct_term.1 = (f32[4,64,128]{2,1,0:T(8,128)S(1)}, bf16[4,64,128]{2,1,0:T(8,128)(2,1)S(1)}) custom-call(f32[4,512,1024]{2,1,0:T(8,128)S(1)} %get-tuple-element.11.refs_0_, bf16[3,512,1024]{2,1,0:T(8,128)(2,1)S(1)} %get-tuple-element.12.refs_1_, bf16[128,512]{1,0:T(8,128)(2,1)S(1)} %get-tuple-element.13.refs_2_, ...), custom_call_target="tpu_custom_call" | custom-call | tf_op jit(solution)/shard_map/direct_term/pallas_call | solution.py:347
  30.3 0.3 collective-permute-start.12
  30.7 1.0 %collective-permute-done.12 = bf16[4,64,128]{2,1,0:T(8,128)(2,1)S(1)} collective-permute-done((bf16[4,64,128]{2,1,0:T(8,128)(2,1)S(1)}, bf16[4,64,128]{2,1,0:T(8,128)(2,1)S(1)}, u32[]{:S(2)}, u32[]{:S(2)}) %collective-permute-start.12) | collective-permute-done | bytes 65568 | tf_op jit(solution)/shard_map/ppermute | solution.py:28
  31.7 2.5 %collective-permute-start.13 = (bf16[4,64,128]{2,1,0:T(8,128)(2,1)S(1)}, bf16[4,64,128]{2,1,0:T(8,128)(2,1)S(1)}, u32[]{:S(2)}, u32[]{:S(2)}) collective-permute-start(bf16[4,64,128]{2,1,0:T(8,128)(2,1)S(1)} %add_convert_fusion), channel_id=1, source_target_pairs={{0,6},{2,4},{4,2},{6,0},{1,7},{3,5},{5,3},{7,1},{8,14},{10,12},{12... | collective-permute-start | bytes 196616 | tf_op jit(solution)/shard_map/ppermute | solution.py:28
  34.2 0.5 %collective-permute-start.15 = (bf16[4,64,128]{2,1,0:T(8,128)(2,1)S(1)}, bf16[4,64,128]{2,1,0:T(8,128)(2,1)S(1)}, u32[]{:S(2)}, u32[]{:S(2)}) collective-permute-start(bf16[4,64,128]{2,1,0:T(8,128)(2,1)S(1)} %add_convert_fusion), channel_id=1, source_target_pairs={{0,2},{2,0},{4,6},{6,4},{1,3},{3,1},{5,7},{7,5},{8,10},{10,8},{12,... | collective-permute-start | bytes 196616 | tf_op jit(solution)/shard_map/ppermute | solution.py:28
  34.7 0.5 %collective-permute-start.14 = (bf16[4,64,128]{2,1,0:T(8,128)(2,1)S(1)}, bf16[4,64,128]{2,1,0:T(8,128)(2,1)S(1)}, u32[]{:S(2)}, u32[]{:S(2)}) collective-permute-start(bf16[4,64,128]{2,1,0:T(8,128)(2,1)S(1)} %add_convert_fusion), channel_id=1, source_target_pairs={{0,4},{2,6},{4,0},{6,2},{1,5},{3,7},{5,1},{7,3},{8,12},{10,14},{12... | collective-permute-start | bytes 196616 | tf_op jit(solution)/shard_map/ppermute | solution.py:28
  35.2 1.9 %collective-permute-done.13.refs_0_ = bf16[4,64,128]{2,1,0:T(8,128)(2,1)S(1)} collective-permute-done((bf16[4,64,128]{2,1,0:T(8,128)(2,1)S(1)}, bf16[4,64,128]{2,1,0:T(8,128)(2,1)S(1)}, u32[]{:S(2)}, u32[]{:S(2)}) %collective-permute-start.13) | collective-permute-done | bytes 65568 | tf_op jit(solution)/shard_map/ppermute | solution.py:28
  37.2 1.3 %collective-permute-done.15 = bf16[4,64,128]{2,1,0:T(8,128)(2,1)S(1)} collective-permute-done((bf16[4,64,128]{2,1,0:T(8,128)(2,1)S(1)}, bf16[4,64,128]{2,1,0:T(8,128)(2,1)S(1)}, u32[]{:S(2)}, u32[]{:S(2)}) %collective-permute-start.15) | collective-permute-done | bytes 65568 | tf_op jit(solution)/shard_map/ppermute | solution.py:28
  38.5 0.5 %collective-permute-done.14 = bf16[4,64,128]{2,1,0:T(8,128)(2,1)S(1)} collective-permute-done((bf16[4,64,128]{2,1,0:T(8,128)(2,1)S(1)}, bf16[4,64,128]{2,1,0:T(8,128)(2,1)S(1)}, u32[]{:S(2)}, u32[]{:S(2)}) %collective-permute-start.14) | collective-permute-done | bytes 65568 | tf_op jit(solution)/shard_map/ppermute | solution.py:28
  39.0 0.7 %add_bitcast_fusion = f32[1,4,64,128]{3,2,1,0:T(8,128)} fusion(bf16[4,64,128]{2,1,0:T(8,128)(2,1)S(1)} %add_convert_fusion, bf16[4,64,128]{2,1,0:T(8,128)(2,1)S(1)} %collective-permute-done.15, bf16[4,64,128]{2,1,0:T(8,128)(2,1)S(1)} %collective-permute-done.14, bf16[4,64,128]{2,1,0:T(8,128)(2,1)S(1)} %after.5), kind=kLoop, calls=%fused_computation | loop fusion | flops 229376 | bytes 393216 | tf_op jit(solution)/shard_map/broadcast_in_dim | solution.py:375
  (5 shorter events, 0.1 us)
Async XLA Ops:
  0.8 5.6 %collective-permute-start = (bf16[32,1024]{1,0:T(8,128)(2,1)S(1)}, bf16[32,1024]{1,0:T(8,128)(2,1)S(1)}, u32[]{:S(2)}, u32[]{:S(2)}) collective-permute-start(bf16[32,1024]{1,0:T(8,128)(2,1)S(1)} %dynamic-slice_bitcast_fusion), channel_id=1, source_target_pairs={{0,8},{8,0},{16,24},{24,16},{1,9},{9,1},{17,25},{25,17},{2,10},{10... | collective-permute-start | bytes 196616 | tf_op jit(solution)/shard_map/ppermute | solution.py:28
  3.9 7.3 %collective-permute-start.1 = (bf16[32,1024]{1,0:T(8,128)(2,1)S(1)}, bf16[32,1024]{1,0:T(8,128)(2,1)S(1)}, u32[]{:S(2)}, u32[]{:S(2)}) collective-permute-start(bf16[32,1024]{1,0:T(8,128)(2,1)S(1)} %dynamic-slice_bitcast_fusion), channel_id=1, source_target_pairs={{0,16},{8,24},{16,0},{24,8},{1,17},{9,25},{17,1},{25,9},{2,18},{10... | collective-permute-start | bytes 196616 | tf_op jit(solution)/shard_map/ppermute | solution.py:28
  6.5 6.8 %collective-permute-start.3 = (bf16[32,1024]{1,0:T(8,128)(2,1)S(1)}, bf16[32,1024]{1,0:T(8,128)(2,1)S(1)}, u32[]{:S(2)}, u32[]{:S(2)}) collective-permute-start(bf16[32,1024]{1,0:T(8,128)(2,1)S(1)} %dynamic-slice_bitcast_fusion), channel_id=1, source_target_pairs={{0,24},{8,16},{16,8},{24,0},{1,25},{9,17},{17,9},{25,1},{2,26},{10... | collective-permute-start | bytes 196616 | tf_op jit(solution)/shard_map/ppermute | solution.py:28
  7.4 11.3 %collective-permute-start.4 = (bf16[512,128]{1,0:T(8,128)(2,1)S(1)}, bf16[512,128]{1,0:T(8,128)(2,1)S(1)}, u32[]{:S(2)}, u32[]{:S(2)}) collective-permute-start(bf16[512,128]{1,0:T(8,128)(2,1)S(1)} %pack.1.refs_0_), channel_id=1, source_target_pairs={{0,8},{8,0},{16,24},{24,16},{1,9},{9,1},{17,25},{25,17},{2,10},{10... | collective-permute-start | bytes 393224 | tf_op jit(solution)/shard_map/ppermute | solution.py:28
  11.2 7.5 %collective-permute-start.2 = (bf16[512,128]{1,0:T(8,128)(2,1)S(1)}, bf16[512,128]{1,0:T(8,128)(2,1)S(1)}, u32[]{:S(2)}, u32[]{:S(2)}) collective-permute-start(bf16[512,128]{1,0:T(8,128)(2,1)S(1)} %after.3), channel_id=1, source_target_pairs={{0,16},{8,24},{16,0},{24,8},{1,17},{9,25},{17,1},{25,9},{2,18},{10... | collective-permute-start | bytes 393224 | tf_op jit(solution)/shard_map/ppermute | solution.py:28
  13.2 9.7 %collective-permute-start.11 = (bf16[96,1024]{1,0:T(8,128)(2,1)S(1)}, bf16[96,1024]{1,0:T(8,128)(2,1)S(1)}, u32[]{:S(2)}, u32[]{:S(2)}) collective-permute-start(bf16[96,1024]{1,0:T(8,128)(2,1)S(1)} %join.1.refs_1_.refs_0_), channel_id=1, source_target_pairs={{0,6},{2,4},{4,2},{6,0},{1,7},{3,5},{5,3},{7,1},{8,14},{10,12},{12... | collective-permute-start | bytes 589832 | tf_op jit(solution)/shard_map/ppermute | solution.py:28
  15.8 8.0 %collective-permute-start.10 = (bf16[96,1024]{1,0:T(8,128)(2,1)S(1)}, bf16[96,1024]{1,0:T(8,128)(2,1)S(1)}, u32[]{:S(2)}, u32[]{:S(2)}) collective-permute-start(bf16[96,1024]{1,0:T(8,128)(2,1)S(1)} %join.1.refs_1_.refs_0_), channel_id=1, source_target_pairs={{0,4},{2,6},{4,0},{6,2},{1,5},{3,7},{5,1},{7,3},{8,12},{10,14},{12... | collective-permute-start | bytes 589832 | tf_op jit(solution)/shard_map/ppermute | solution.py:28
  16.3 7.5 %collective-permute-start.9 = (bf16[96,1024]{1,0:T(8,128)(2,1)S(1)}, bf16[96,1024]{1,0:T(8,128)(2,1)S(1)}, u32[]{:S(2)}, u32[]{:S(2)}) collective-permute-start(bf16[96,1024]{1,0:T(8,128)(2,1)S(1)} %join.1.refs_1_.refs_0_), channel_id=1, source_target_pairs={{0,2},{2,0},{4,6},{6,4},{1,3},{3,1},{5,7},{7,5},{8,10},{10,8},{12,... | collective-permute-start | bytes 589832 | tf_op jit(solution)/shard_map/ppermute | solution.py:28
  18.7 5.0 %collective-permute-start.7 = (bf16[512,128]{1,0:T(8,128)(2,1)S(1)}, bf16[512,128]{1,0:T(8,128)(2,1)S(1)}, u32[]{:S(2)}, u32[]{:S(2)}) collective-permute-start(bf16[512,128]{1,0:T(8,128)(2,1)S(1)} %after.4.after_ref.refs_2_), channel_id=1, source_target_pairs={{0,8},{8,0},{16,24},{24,16},{1,9},{9,1},{17,25},{25,17},{2,10},{10... | collective-permute-start | bytes 393224 | tf_op jit(solution)/shard_map/ppermute | solution.py:28
  18.8 5.0 %collective-permute-start.6 = (bf16[512,128]{1,0:T(8,128)(2,1)S(1)}, bf16[512,128]{1,0:T(8,128)(2,1)S(1)}, u32[]{:S(2)}, u32[]{:S(2)}) collective-permute-start(bf16[512,128]{1,0:T(8,128)(2,1)S(1)} %after.4.after_ref.refs_2_), channel_id=1, source_target_pairs={{0,1},{1,0},{2,3},{3,2},{4,5},{5,4},{6,7},{7,6},{8,9},{9,8},{10,11... | collective-permute-start | bytes 393224 | tf_op jit(solution)/shard_map/ppermute | solution.py:28
  22.9 1.5 %collective-permute-start.5 = (bf16[512,128]{1,0:T(8,128)(2,1)S(1)}, bf16[512,128]{1,0:T(8,128)(2,1)S(1)}, u32[]{:S(2)}, u32[]{:S(2)}) collective-permute-start(bf16[512,128]{1,0:T(8,128)(2,1)S(1)} %collective-permute-done.4.refs_2_.refs_0_), channel_id=1, source_target_pairs={{0,1},{1,0},{2,3},{3,2},{4,5},{5,4},{6,7},{7,6},{8,9},{9,8},{10,11... | collective-permute-start | bytes 393224 | tf_op jit(solution)/shard_map/ppermute | solution.py:28
  23.7 1.3 %collective-permute-start.8 = (bf16[512,128]{1,0:T(8,128)(2,1)S(1)}, bf16[512,128]{1,0:T(8,128)(2,1)S(1)}, u32[]{:S(2)}, u32[]{:S(2)}) collective-permute-start(bf16[512,128]{1,0:T(8,128)(2,1)S(1)} %collective-permute-done.7.refs_5_), channel_id=1, source_target_pairs={{0,1},{1,0},{2,3},{3,2},{4,5},{5,4},{6,7},{7,6},{8,9},{9,8},{10,11... | collective-permute-start | bytes 393224 | tf_op jit(solution)/shard_map/ppermute | solution.py:28
  30.3 1.3 %collective-permute-start.12 = (bf16[4,64,128]{2,1,0:T(8,128)(2,1)S(1)}, bf16[4,64,128]{2,1,0:T(8,128)(2,1)S(1)}, u32[]{:S(2)}, u32[]{:S(2)}) collective-permute-start(bf16[4,64,128]{2,1,0:T(8,128)(2,1)S(1)} %get-tuple-element.16), channel_id=1, source_target_pairs={{0,1},{1,0},{2,3},{3,2},{4,5},{5,4},{6,7},{7,6},{8,9},{9,8},{10,11... | collective-permute-start | bytes 196616 | tf_op jit(solution)/shard_map/ppermute | solution.py:28
  31.7 5.5 %collective-permute-start.13 = (bf16[4,64,128]{2,1,0:T(8,128)(2,1)S(1)}, bf16[4,64,128]{2,1,0:T(8,128)(2,1)S(1)}, u32[]{:S(2)}, u32[]{:S(2)}) collective-permute-start(bf16[4,64,128]{2,1,0:T(8,128)(2,1)S(1)} %add_convert_fusion), channel_id=1, source_target_pairs={{0,6},{2,4},{4,2},{6,0},{1,7},{3,5},{5,3},{7,1},{8,14},{10,12},{12... | collective-permute-start | bytes 196616 | tf_op jit(solution)/shard_map/ppermute | solution.py:28
  34.2 4.3 %collective-permute-start.15 = (bf16[4,64,128]{2,1,0:T(8,128)(2,1)S(1)}, bf16[4,64,128]{2,1,0:T(8,128)(2,1)S(1)}, u32[]{:S(2)}, u32[]{:S(2)}) collective-permute-start(bf16[4,64,128]{2,1,0:T(8,128)(2,1)S(1)} %add_convert_fusion), channel_id=1, source_target_pairs={{0,2},{2,0},{4,6},{6,4},{1,3},{3,1},{5,7},{7,5},{8,10},{10,8},{12,... | collective-permute-start | bytes 196616 | tf_op jit(solution)/shard_map/ppermute | solution.py:28
  34.7 4.3 %collective-permute-start.14 = (bf16[4,64,128]{2,1,0:T(8,128)(2,1)S(1)}, bf16[4,64,128]{2,1,0:T(8,128)(2,1)S(1)}, u32[]{:S(2)}, u32[]{:S(2)}) collective-permute-start(bf16[4,64,128]{2,1,0:T(8,128)(2,1)S(1)} %add_convert_fusion), channel_id=1, source_target_pairs={{0,4},{2,6},{4,0},{6,2},{1,5},{3,7},{5,1},{7,3},{8,12},{10,14},{12... | collective-permute-start | bytes 196616 | tf_op jit(solution)/shard_map/ppermute | solution.py:28
where the time goes:
time: 39.9 us; the launch traced here: 39.7 us
  starting transfers between devices  16.8 us (42%)
  Pallas kernels  10.9 us (27%)
  waiting for transfers between devices  10.4 us (26%)
  local copies, waits for them, and re-layouts  0.84 us (2%)
  other arithmetic  0.71 us (2%)
    ppermute x16, starting transfers between devices, swap(): return lax.ppermute(value, axis, [(i, i ^ flip) for i in range(size)])  16.8 us
    ppermute x16, waiting for transfers between devices, swap(): return lax.ppermute(value, axis, [(i, i ^ flip) for i in range(size)])  10.4 us
    pallas_call x1, Pallas kernels, local(): pl.pallas_call(functools.partial(direct_kernel, sizes, early, factor), in...  5.24 us
    pallas_call x1, Pallas kernels, local(): pl.pallas_call(own_kernel, in_specs=[IN_SMEM] + [IN_HBM] * 4 + [pl.BlockS...  4.06 us
    pallas_call x1, Pallas kernels, local(): pl.pallas_call(functools.partial(pack_kernel, n_col), in_specs=[IN_HBM] *...  0.95 us
    dynamic_slice x1, local copies, waits for them, and re-layouts, local(): lax.dynamic_slice_in_dim(orb_val[0], lax.axis_index('row') * part, part, 0)  0.84 us
  transfers between devices with their start and end apart: 16, of which 10 were waited for; matrix products, arithmetic and copies ran while one was open for 0% of the time, Pallas kernels for 14%

commit v1 on v0

--- a/solution.py
+++ b/solution.py
@@ -173,7 +173,7 @@
     cores = [take(n_col) for _ in late]
     val_ref, = take(1)
     keep, *sent = take(n_col)
-    x_all, cond_all, panels, products, direct, running, half, total = refs
+    x_all, cond_all, panels, products, direct, running, total, result = refs
     col = lax.axis_index("col")
     n_v, n_nu = val_own.shape
     n_c, n_mu = cond_own.shape
@@ -227,7 +227,11 @@
             return
         value = value.astype(BF16)
         for b in range(n_b):
-            half[b, t * TILE:(t + 1) * TILE, :] = value[b * TILE:(b + 1) * TILE, :]
+            part = jnp.dot(
+                cond_own[:, t * TILE:(t + 1) * TILE], value[b * TILE:(b + 1) * TILE, :],
+                preferred_element_type=F32,
+            )
+            total[b] = total[b] + part if t else part
 
     all_panels(0)
     for i in range(n_others):
@@ -241,20 +245,19 @@
                 multiply(number + 1, i)
             if i < QUARTERS:
                 combine(number, i)
-        reduce(number)
+            if i == 0 and number:
+                reduce(number - 1)
+    reduce(len(steps) - 1)
 
     part = n_v // n_col
     for b in range(n_b):
-        total[b * n_v:(b + 1) * n_v, :] = (
-            jnp.dot(cond_own[...], half[b], preferred_element_type=F32) * factor
-        ).T
+        result[...] = (total[b] * factor).T
         for other in range(n_col):
-            rows = pl.ds(pl.multiple_of(b * n_v + (col ^ other) * part, part), part)
-            value = total[rows, :]
+            rows = pl.ds(pl.multiple_of((col ^ other) * part, part), part)
             if other == 0:
-                keep[b] = value
+                keep[b] = result[rows, :]
             else:
-                sent[other - 1][b] = value.astype(BF16)
+                sent[other - 1][b] = result[rows, :].astype(BF16)
 
 
 def local(sizes, exciton, orb_cond, orb_val, screened, q_table):
@@ -357,8 +360,8 @@
             pltpu.VMEM((2, n_ka - 1, n_b * TILE, CHUNK), BF16),
             pltpu.VMEM((2, n_b * TILE, n_nu), BF16),
             pltpu.VMEM((n_b * TILE, n_v), F32),
-            pltpu.VMEM((n_b, n_mu, n_v), BF16),
-            pltpu.VMEM((n_b * n_v, n_c), F32),
+            pltpu.VMEM((n_b, n_c, n_v), F32),
+            pltpu.VMEM((n_v, n_c), F32),
         ],
         compiler_params=pltpu.CompilerParams(vmem_limit_bytes=36 * MIB),
         name="direct_term",

time: 39.9 us -> 40.5 us (1.015)
  Pallas kernels: 10.9 us -> 11.4 us
    pallas_call x1, Pallas kernels: 5.24 us -> 5.81 us  [local(): pl.pallas_call(functools.partial(direct_kernel, sizes, early, factor), in...]
where the time goes in v1:
time: 40.5 us; the launch traced here: 40.3 us
  starting transfers between devices  16.8 us (41%)
  Pallas kernels  11.4 us (28%)
  waiting for transfers between devices  10.4 us (26%)
  local copies, waits for them, and re-layouts  0.84 us (2%)
  other arithmetic  0.71 us (2%)
    ppermute x16, starting transfers between devices, swap(): return lax.ppermute(value, axis, [(i, i ^ flip) for i in range(size)])  16.8 us
    ppermute x16, waiting for transfers between devices, swap(): return lax.ppermute(value, axis, [(i, i ^ flip) for i in range(size)])  10.4 us
    pallas_call x1, Pallas kernels, local(): pl.pallas_call(functools.partial(direct_kernel, sizes, early, factor), in...  5.81 us
    pallas_call x1, Pallas kernels, local(): pl.pallas_call(own_kernel, in_specs=[IN_SMEM] + [IN_HBM] * 4 + [pl.BlockS...  4.06 us
    pallas_call x1, Pallas kernels, local(): pl.pallas_call(functools.partial(pack_kernel, n_col), in_specs=[IN_HBM] *...  0.95 us
    dynamic_slice x1, local copies, waits for them, and re-layouts, local(): lax.dynamic_slice_in_dim(orb_val[0], lax.axis_index('row') * part, part, 0)  0.84 us
  transfers between devices with their start and end apart: 16, of which 10 were waited for; matrix products, arithmetic and copies ran while one was open for 0% of the time, Pallas kernels for 14%

profile of v1, /device:TPU:0, one launch (start us, length us, event | category | flops | bytes accessed | tf_op | source)
XLA Modules:
  0.0 40.3 jit_solution(5309475196679279921)
XLA Ops:
  0.0 0.8 %dynamic-slice_bitcast_fusion = bf16[32,1024]{1,0:T(8,128)(2,1)S(1)} fusion(bf16[1,128,1024]{2,1,0:T(8,128)(2,1)} %param.7, s32[]{:T(128)S(6)} %select_n.3), kind=kLoop, calls=%fused_computation.2 | loop fusion | bytes 131076 | tf_op jit(solution)/shard_map/dynamic_slice | solution.py:273
  0.8 3.0 %collective-permute-start = (bf16[32,1024]{1,0:T(8,128)(2,1)S(1)}, bf16[32,1024]{1,0:T(8,128)(2,1)S(1)}, u32[]{:S(2)}, u32[]{:S(2)}) collective-permute-start(bf16[32,1024]{1,0:T(8,128)(2,1)S(1)} %dynamic-slice_bitcast_fusion), channel_id=1, source_target_pairs={{0,8},{8,0},{16,24},{24,16},{1,9},{9,1},{17,25},{25,17},{2,10},{10... | collective-permute-start | bytes 196616 | tf_op jit(solution)/shard_map/ppermute | solution.py:28
  3.9 2.6 %collective-permute-start.1 = (bf16[32,1024]{1,0:T(8,128)(2,1)S(1)}, bf16[32,1024]{1,0:T(8,128)(2,1)S(1)}, u32[]{:S(2)}, u32[]{:S(2)}) collective-permute-start(bf16[32,1024]{1,0:T(8,128)(2,1)S(1)} %dynamic-slice_bitcast_fusion), channel_id=1, source_target_pairs={{0,16},{8,24},{16,0},{24,8},{1,17},{9,25},{17,1},{25,9},{2,18},{10... | collective-permute-start | bytes 196616 | tf_op jit(solution)/shard_map/ppermute | solution.py:28
  6.5 0.0 collective-permute-start.3
  6.5 0.0 collective-permute-done.after_ref.refs_0_
  6.5 1.0 %pack.1.refs_0_ = bf16[512,128]{1,0:T(8,128)(2,1)S(1)} custom-call(bf16[512,128]{1,0:T(8,128)(2,1)} %bitcast.7, bf16[128,512]{1,0:T(8,128)(2,1)} %bitcast.9, bf16[32,1024]{1,0:T(8,128)(2,1)S(1)} %collective-permute-done.after_ref.refs_0_), custom_call_target="tpu_custom_call" | custom-call | tf_op jit(solution)/shard_map/pack/pallas_call | solution.py:275
  7.4 1.7 %collective-permute-start.4 = (bf16[512,128]{1,0:T(8,128)(2,1)S(1)}, bf16[512,128]{1,0:T(8,128)(2,1)S(1)}, u32[]{:S(2)}, u32[]{:S(2)}) collective-permute-start(bf16[512,128]{1,0:T(8,128)(2,1)S(1)} %pack.1.refs_0_), channel_id=1, source_target_pairs={{0,8},{8,0},{16,24},{24,16},{1,9},{9,1},{17,25},{25,17},{2,10},{10... | collective-permute-start | bytes 393224 | tf_op jit(solution)/shard_map/ppermute | solution.py:28
  9.2 2.0 %collective-permute-done.1.refs_1_ = bf16[32,1024]{1,0:T(8,128)(2,1)S(1)} collective-permute-done((bf16[32,1024]{1,0:T(8,128)(2,1)S(1)}, bf16[32,1024]{1,0:T(8,128)(2,1)S(1)}, u32[]{:S(2)}, u32[]{:S(2)}) %collective-permute-start.1) | collective-permute-done | bytes 65568 | tf_op jit(solution)/shard_map/ppermute | solution.py:28
  11.2 1.3 %collective-permute-start.2 = (bf16[512,128]{1,0:T(8,128)(2,1)S(1)}, bf16[512,128]{1,0:T(8,128)(2,1)S(1)}, u32[]{:S(2)}, u32[]{:S(2)}) collective-permute-start(bf16[512,128]{1,0:T(8,128)(2,1)S(1)} %after.3), channel_id=1, source_target_pairs={{0,16},{8,24},{16,0},{24,8},{1,17},{9,25},{17,1},{25,9},{2,18},{10... | collective-permute-start | bytes 393224 | tf_op jit(solution)/shard_map/ppermute | solution.py:28
  12.5 0.8 %collective-permute-done.3.refs_2_ = bf16[32,1024]{1,0:T(8,128)(2,1)S(1)} collective-permute-done((bf16[32,1024]{1,0:T(8,128)(2,1)S(1)}, bf16[32,1024]{1,0:T(8,128)(2,1)S(1)}, u32[]{:S(2)}, u32[]{:S(2)}) %collective-permute-start.3) | collective-permute-done | bytes 65568 | tf_op jit(solution)/shard_map/ppermute | solution.py:28
  13.2 2.5 %collective-permute-start.11 = (bf16[96,1024]{1,0:T(8,128)(2,1)S(1)}, bf16[96,1024]{1,0:T(8,128)(2,1)S(1)}, u32[]{:S(2)}, u32[]{:S(2)}) collective-permute-start(bf16[96,1024]{1,0:T(8,128)(2,1)S(1)} %join.1.refs_1_.refs_0_), channel_id=1, source_target_pairs={{0,6},{2,4},{4,2},{6,0},{1,7},{3,5},{5,3},{7,1},{8,14},{10,12},{12... | collective-permute-start | bytes 589832 | tf_op jit(solution)/shard_map/ppermute | solution.py:28
  15.8 0.5 %collective-permute-start.10 = (bf16[96,1024]{1,0:T(8,128)(2,1)S(1)}, bf16[96,1024]{1,0:T(8,128)(2,1)S(1)}, u32[]{:S(2)}, u32[]{:S(2)}) collective-permute-start(bf16[96,1024]{1,0:T(8,128)(2,1)S(1)} %join.1.refs_1_.refs_0_), channel_id=1, source_target_pairs={{0,4},{2,6},{4,0},{6,2},{1,5},{3,7},{5,1},{7,3},{8,12},{10,14},{12... | collective-permute-start | bytes 589832 | tf_op jit(solution)/shard_map/ppermute | solution.py:28
  16.3 0.5 %collective-permute-start.9 = (bf16[96,1024]{1,0:T(8,128)(2,1)S(1)}, bf16[96,1024]{1,0:T(8,128)(2,1)S(1)}, u32[]{:S(2)}, u32[]{:S(2)}) collective-permute-start(bf16[96,1024]{1,0:T(8,128)(2,1)S(1)} %join.1.refs_1_.refs_0_), channel_id=1, source_target_pairs={{0,2},{2,0},{4,6},{6,4},{1,3},{3,1},{5,7},{7,5},{8,10},{10,8},{12,... | collective-permute-start | bytes 589832 | tf_op jit(solution)/shard_map/ppermute | solution.py:28
  16.8 1.9 %collective-permute-done.2.refs_0_ = bf16[512,128]{1,0:T(8,128)(2,1)S(1)} collective-permute-done((bf16[512,128]{1,0:T(8,128)(2,1)S(1)}, bf16[512,128]{1,0:T(8,128)(2,1)S(1)}, u32[]{:S(2)}, u32[]{:S(2)}) %collective-permute-start.2) | collective-permute-done | bytes 131104 | tf_op jit(solution)/shard_map/ppermute | solution.py:28
  18.7 0.0 collective-permute-done.4.refs_2_.refs_0_
  18.7 0.1 collective-permute-start.7
  18.8 0.1 collective-permute-start.6
  18.9 4.1 %own_term.1 = (f32[4,512,1024]{2,1,0:T(8,128)S(1)}, bf16[3,512,1024]{2,1,0:T(8,128)(2,1)S(1)}, bf16[128,512]{1,0:T(8,128)(2,1)S(1)}, bf16[128,1024]{1,0:T(8,128)(2,1)S(1)}) custom-call(s32[4,4]{1,0:T(4,128)} %q_ref.1, bf16[4,512,1024]{2,1,0:T(8,128)(2,1)} %w_ref.1, bf16[512,128]{1,0:T(8,128)(2,1)} %bitcast.8, bf16[128,512]{1,0:T(8,128)(2,1)} %bitcast.10, ...), custom_call_target="tpu_custom_call" | custom-call | bytes 8388608 | tf_op jit(solution)/shard_map/own_term/pallas_call | solution.py:295
  22.9 0.0 collective-permute-done.11.refs_3_
  22.9 0.6 %collective-permute-start.5 = (bf16[512,128]{1,0:T(8,128)(2,1)S(1)}, bf16[512,128]{1,0:T(8,128)(2,1)S(1)}, u32[]{:S(2)}, u32[]{:S(2)}) collective-permute-start(bf16[512,128]{1,0:T(8,128)(2,1)S(1)} %collective-permute-done.4.refs_2_.refs_0_), channel_id=1, source_target_pairs={{0,1},{1,0},{2,3},{3,2},{4,5},{5,4},{6,7},{7,6},{8,9},{9,8},{10,11... | collective-permute-start | bytes 393224 | tf_op jit(solution)/shard_map/ppermute | solution.py:28
  23.5 0.2 collective-permute-done.7.refs_5_
  23.7 0.0 collective-permute-start.8
  23.7 0.0 collective-permute-done.10.refs_2_
  23.7 0.0 collective-permute-done.9.refs_1_
  23.7 0.1 spread.1.refs_7_
  23.8 0.0 collective-permute-done.6.refs_3_
  23.8 0.6 %collective-permute-done.5.refs_1_ = bf16[512,128]{1,0:T(8,128)(2,1)S(1)} collective-permute-done((bf16[512,128]{1,0:T(8,128)(2,1)S(1)}, bf16[512,128]{1,0:T(8,128)(2,1)S(1)}, u32[]{:S(2)}, u32[]{:S(2)}) %collective-permute-start.5) | collective-permute-done | bytes 131104 | tf_op jit(solution)/shard_map/ppermute | solution.py:28
  24.5 0.5 %panels.1.refs_4_ = bf16[2,4,512,128]{3,2,1,0:T(8,128)(2,1)S(1)} custom-call(bf16[512,128]{1,0:T(8,128)(2,1)S(1)} %collective-permute-done.4.refs_2_.refs_0_, bf16[512,128]{1,0:T(8,128)(2,1)S(1)} %collective-permute-done.5.refs_1_, bf16[512,128]{1,0:T(8,128)(2,1)S(1)} %after.4.after_ref.refs_2_, bf16[512,128]{1,0:T(8,128)(2,1)S(1)} %collective-permute-done.6.refs_3_), custom_call_target="tpu_custom_call" | custom-call | flops 1000000000 | tf_op jit(solution)/shard_map/panels/pallas_call | solution.py:322
  25.0 0.1 collective-permute-done.8.refs_6_
  25.1 5.8 %direct_term.1 = (f32[4,64,128]{2,1,0:T(8,128)S(1)}, bf16[4,64,128]{2,1,0:T(8,128)(2,1)S(1)}) custom-call(f32[4,512,1024]{2,1,0:T(8,128)S(1)} %get-tuple-element.11.refs_0_, bf16[3,512,1024]{2,1,0:T(8,128)(2,1)S(1)} %get-tuple-element.12.refs_1_, bf16[128,512]{1,0:T(8,128)(2,1)S(1)} %get-tuple-element.13.refs_2_, ...), custom_call_target="tpu_custom_call" | custom-call | tf_op jit(solution)/shard_map/direct_term/pallas_call | solution.py:350
  30.9 0.3 collective-permute-start.12
  31.2 1.0 %collective-permute-done.12 = bf16[4,64,128]{2,1,0:T(8,128)(2,1)S(1)} collective-permute-done((bf16[4,64,128]{2,1,0:T(8,128)(2,1)S(1)}, bf16[4,64,128]{2,1,0:T(8,128)(2,1)S(1)}, u32[]{:S(2)}, u32[]{:S(2)}) %collective-permute-start.12) | collective-permute-done | bytes 65568 | tf_op jit(solution)/shard_map/ppermute | solution.py:28
  32.2 2.5 %collective-permute-start.13 = (bf16[4,64,128]{2,1,0:T(8,128)(2,1)S(1)}, bf16[4,64,128]{2,1,0:T(8,128)(2,1)S(1)}, u32[]{:S(2)}, u32[]{:S(2)}) collective-permute-start(bf16[4,64,128]{2,1,0:T(8,128)(2,1)S(1)} %add_convert_fusion), channel_id=1, source_target_pairs={{0,6},{2,4},{4,2},{6,0},{1,7},{3,5},{5,3},{7,1},{8,14},{10,12},{12... | collective-permute-start | bytes 196616 | tf_op jit(solution)/shard_map/ppermute | solution.py:28
  34.8 0.5 %collective-permute-start.15 = (bf16[4,64,128]{2,1,0:T(8,128)(2,1)S(1)}, bf16[4,64,128]{2,1,0:T(8,128)(2,1)S(1)}, u32[]{:S(2)}, u32[]{:S(2)}) collective-permute-start(bf16[4,64,128]{2,1,0:T(8,128)(2,1)S(1)} %add_convert_fusion), channel_id=1, source_target_pairs={{0,2},{2,0},{4,6},{6,4},{1,3},{3,1},{5,7},{7,5},{8,10},{10,8},{12,... | collective-permute-start | bytes 196616 | tf_op jit(solution)/shard_map/ppermute | solution.py:28
  35.3 0.5 %collective-permute-start.14 = (bf16[4,64,128]{2,1,0:T(8,128)(2,1)S(1)}, bf16[4,64,128]{2,1,0:T(8,128)(2,1)S(1)}, u32[]{:S(2)}, u32[]{:S(2)}) collective-permute-start(bf16[4,64,128]{2,1,0:T(8,128)(2,1)S(1)} %add_convert_fusion), channel_id=1, source_target_pairs={{0,4},{2,6},{4,0},{6,2},{1,5},{3,7},{5,1},{7,3},{8,12},{10,14},{12... | collective-permute-start | bytes 196616 | tf_op jit(solution)/shard_map/ppermute | solution.py:28
  35.8 1.9 %collective-permute-done.13.refs_0_ = bf16[4,64,128]{2,1,0:T(8,128)(2,1)S(1)} collective-permute-done((bf16[4,64,128]{2,1,0:T(8,128)(2,1)S(1)}, bf16[4,64,128]{2,1,0:T(8,128)(2,1)S(1)}, u32[]{:S(2)}, u32[]{:S(2)}) %collective-permute-start.13) | collective-permute-done | bytes 65568 | tf_op jit(solution)/shard_map/ppermute | solution.py:28
  37.7 1.3 %collective-permute-done.15 = bf16[4,64,128]{2,1,0:T(8,128)(2,1)S(1)} collective-permute-done((bf16[4,64,128]{2,1,0:T(8,128)(2,1)S(1)}, bf16[4,64,128]{2,1,0:T(8,128)(2,1)S(1)}, u32[]{:S(2)}, u32[]{:S(2)}) %collective-permute-start.15) | collective-permute-done | bytes 65568 | tf_op jit(solution)/shard_map/ppermute | solution.py:28
  39.0 0.5 %collective-permute-done.14 = bf16[4,64,128]{2,1,0:T(8,128)(2,1)S(1)} collective-permute-done((bf16[4,64,128]{2,1,0:T(8,128)(2,1)S(1)}, bf16[4,64,128]{2,1,0:T(8,128)(2,1)S(1)}, u32[]{:S(2)}, u32[]{:S(2)}) %collective-permute-start.14) | collective-permute-done | bytes 65568 | tf_op jit(solution)/shard_map/ppermute | solution.py:28
  39.6 0.7 %add_bitcast_fusion = f32[1,4,64,128]{3,2,1,0:T(8,128)} fusion(bf16[4,64,128]{2,1,0:T(8,128)(2,1)S(1)} %add_convert_fusion, bf16[4,64,128]{2,1,0:T(8,128)(2,1)S(1)} %collective-permute-done.15, bf16[4,64,128]{2,1,0:T(8,128)(2,1)S(1)} %collective-permute-done.14, bf16[4,64,128]{2,1,0:T(8,128)(2,1)S(1)} %after.5), kind=kLoop, calls=%fused_computation | loop fusion | flops 229376 | bytes 393216 | tf_op jit(solution)/shard_map/broadcast_in_dim | solution.py:378
  (5 shorter events, 0.1 us)
Async XLA Ops:
  0.8 5.6 %collective-permute-start = (bf16[32,1024]{1,0:T(8,128)(2,1)S(1)}, bf16[32,1024]{1,0:T(8,128)(2,1)S(1)}, u32[]{:S(2)}, u32[]{:S(2)}) collective-permute-start(bf16[32,1024]{1,0:T(8,128)(2,1)S(1)} %dynamic-slice_bitcast_fusion), channel_id=1, source_target_pairs={{0,8},{8,0},{16,24},{24,16},{1,9},{9,1},{17,25},{25,17},{2,10},{10... | collective-permute-start | bytes 196616 | tf_op jit(solution)/shard_map/ppermute | solution.py:28
  3.9 7.3 %collective-permute-start.1 = (bf16[32,1024]{1,0:T(8,128)(2,1)S(1)}, bf16[32,1024]{1,0:T(8,128)(2,1)S(1)}, u32[]{:S(2)}, u32[]{:S(2)}) collective-permute-start(bf16[32,1024]{1,0:T(8,128)(2,1)S(1)} %dynamic-slice_bitcast_fusion), channel_id=1, source_target_pairs={{0,16},{8,24},{16,0},{24,8},{1,17},{9,25},{17,1},{25,9},{2,18},{10... | collective-permute-start | bytes 196616 | tf_op jit(solution)/shard_map/ppermute | solution.py:28
  6.5 6.8 %collective-permute-start.3 = (bf16[32,1024]{1,0:T(8,128)(2,1)S(1)}, bf16[32,1024]{1,0:T(8,128)(2,1)S(1)}, u32[]{:S(2)}, u32[]{:S(2)}) collective-permute-start(bf16[32,1024]{1,0:T(8,128)(2,1)S(1)} %dynamic-slice_bitcast_fusion), channel_id=1, source_target_pairs={{0,24},{8,16},{16,8},{24,0},{1,25},{9,17},{17,9},{25,1},{2,26},{10... | collective-permute-start | bytes 196616 | tf_op jit(solution)/shard_map/ppermute | solution.py:28
  7.4 11.3 %collective-permute-start.4 = (bf16[512,128]{1,0:T(8,128)(2,1)S(1)}, bf16[512,128]{1,0:T(8,128)(2,1)S(1)}, u32[]{:S(2)}, u32[]{:S(2)}) collective-permute-start(bf16[512,128]{1,0:T(8,128)(2,1)S(1)} %pack.1.refs_0_), channel_id=1, source_target_pairs={{0,8},{8,0},{16,24},{24,16},{1,9},{9,1},{17,25},{25,17},{2,10},{10... | collective-permute-start | bytes 393224 | tf_op jit(solution)/shard_map/ppermute | solution.py:28
  11.2 7.5 %collective-permute-start.2 = (bf16[512,128]{1,0:T(8,128)(2,1)S(1)}, bf16[512,128]{1,0:T(8,128)(2,1)S(1)}, u32[]{:S(2)}, u32[]{:S(2)}) collective-permute-start(bf16[512,128]{1,0:T(8,128)(2,1)S(1)} %after.3), channel_id=1, source_target_pairs={{0,16},{8,24},{16,0},{24,8},{1,17},{9,25},{17,1},{25,9},{2,18},{10... | collective-permute-start | bytes 393224 | tf_op jit(solution)/shard_map/ppermute | solution.py:28
  13.2 9.7 %collective-permute-start.11 = (bf16[96,1024]{1,0:T(8,128)(2,1)S(1)}, bf16[96,1024]{1,0:T(8,128)(2,1)S(1)}, u32[]{:S(2)}, u32[]{:S(2)}) collective-permute-start(bf16[96,1024]{1,0:T(8,128)(2,1)S(1)} %join.1.refs_1_.refs_0_), channel_id=1, source_target_pairs={{0,6},{2,4},{4,2},{6,0},{1,7},{3,5},{5,3},{7,1},{8,14},{10,12},{12... | collective-permute-start | bytes 589832 | tf_op jit(solution)/shard_map/ppermute | solution.py:28
  15.8 8.0 %collective-permute-start.10 = (bf16[96,1024]{1,0:T(8,128)(2,1)S(1)}, bf16[96,1024]{1,0:T(8,128)(2,1)S(1)}, u32[]{:S(2)}, u32[]{:S(2)}) collective-permute-start(bf16[96,1024]{1,0:T(8,128)(2,1)S(1)} %join.1.refs_1_.refs_0_), channel_id=1, source_target_pairs={{0,4},{2,6},{4,0},{6,2},{1,5},{3,7},{5,1},{7,3},{8,12},{10,14},{12... | collective-permute-start | bytes 589832 | tf_op jit(solution)/shard_map/ppermute | solution.py:28
  16.3 7.5 %collective-permute-start.9 = (bf16[96,1024]{1,0:T(8,128)(2,1)S(1)}, bf16[96,1024]{1,0:T(8,128)(2,1)S(1)}, u32[]{:S(2)}, u32[]{:S(2)}) collective-permute-start(bf16[96,1024]{1,0:T(8,128)(2,1)S(1)} %join.1.refs_1_.refs_0_), channel_id=1, source_target_pairs={{0,2},{2,0},{4,6},{6,4},{1,3},{3,1},{5,7},{7,5},{8,10},{10,8},{12,... | collective-permute-start | bytes 589832 | tf_op jit(solution)/shard_map/ppermute | solution.py:28
  18.7 5.0 %collective-permute-start.7 = (bf16[512,128]{1,0:T(8,128)(2,1)S(1)}, bf16[512,128]{1,0:T(8,128)(2,1)S(1)}, u32[]{:S(2)}, u32[]{:S(2)}) collective-permute-start(bf16[512,128]{1,0:T(8,128)(2,1)S(1)} %after.4.after_ref.refs_2_), channel_id=1, source_target_pairs={{0,8},{8,0},{16,24},{24,16},{1,9},{9,1},{17,25},{25,17},{2,10},{10... | collective-permute-start | bytes 393224 | tf_op jit(solution)/shard_map/ppermute | solution.py:28
  18.8 5.0 %collective-permute-start.6 = (bf16[512,128]{1,0:T(8,128)(2,1)S(1)}, bf16[512,128]{1,0:T(8,128)(2,1)S(1)}, u32[]{:S(2)}, u32[]{:S(2)}) collective-permute-start(bf16[512,128]{1,0:T(8,128)(2,1)S(1)} %after.4.after_ref.refs_2_), channel_id=1, source_target_pairs={{0,1},{1,0},{2,3},{3,2},{4,5},{5,4},{6,7},{7,6},{8,9},{9,8},{10,11... | collective-permute-start | bytes 393224 | tf_op jit(solution)/shard_map/ppermute | solution.py:28
  22.9 1.5 %collective-permute-start.5 = (bf16[512,128]{1,0:T(8,128)(2,1)S(1)}, bf16[512,128]{1,0:T(8,128)(2,1)S(1)}, u32[]{:S(2)}, u32[]{:S(2)}) collective-permute-start(bf16[512,128]{1,0:T(8,128)(2,1)S(1)} %collective-permute-done.4.refs_2_.refs_0_), channel_id=1, source_target_pairs={{0,1},{1,0},{2,3},{3,2},{4,5},{5,4},{6,7},{7,6},{8,9},{9,8},{10,11... | collective-permute-start | bytes 393224 | tf_op jit(solution)/shard_map/ppermute | solution.py:28
  23.7 1.3 %collective-permute-start.8 = (bf16[512,128]{1,0:T(8,128)(2,1)S(1)}, bf16[512,128]{1,0:T(8,128)(2,1)S(1)}, u32[]{:S(2)}, u32[]{:S(2)}) collective-permute-start(bf16[512,128]{1,0:T(8,128)(2,1)S(1)} %collective-permute-done.7.refs_5_), channel_id=1, source_target_pairs={{0,1},{1,0},{2,3},{3,2},{4,5},{5,4},{6,7},{7,6},{8,9},{9,8},{10,11... | collective-permute-start | bytes 393224 | tf_op jit(solution)/shard_map/ppermute | solution.py:28
  30.9 1.3 %collective-permute-start.12 = (bf16[4,64,128]{2,1,0:T(8,128)(2,1)S(1)}, bf16[4,64,128]{2,1,0:T(8,128)(2,1)S(1)}, u32[]{:S(2)}, u32[]{:S(2)}) collective-permute-start(bf16[4,64,128]{2,1,0:T(8,128)(2,1)S(1)} %get-tuple-element.16), channel_id=1, source_target_pairs={{0,1},{1,0},{2,3},{3,2},{4,5},{5,4},{6,7},{7,6},{8,9},{9,8},{10,11... | collective-permute-start | bytes 196616 | tf_op jit(solution)/shard_map/ppermute | solution.py:28
  32.2 5.5 %collective-permute-start.13 = (bf16[4,64,128]{2,1,0:T(8,128)(2,1)S(1)}, bf16[4,64,128]{2,1,0:T(8,128)(2,1)S(1)}, u32[]{:S(2)}, u32[]{:S(2)}) collective-permute-start(bf16[4,64,128]{2,1,0:T(8,128)(2,1)S(1)} %add_convert_fusion), channel_id=1, source_target_pairs={{0,6},{2,4},{4,2},{6,0},{1,7},{3,5},{5,3},{7,1},{8,14},{10,12},{12... | collective-permute-start | bytes 196616 | tf_op jit(solution)/shard_map/ppermute | solution.py:28
  34.8 4.3 %collective-permute-start.15 = (bf16[4,64,128]{2,1,0:T(8,128)(2,1)S(1)}, bf16[4,64,128]{2,1,0:T(8,128)(2,1)S(1)}, u32[]{:S(2)}, u32[]{:S(2)}) collective-permute-start(bf16[4,64,128]{2,1,0:T(8,128)(2,1)S(1)} %add_convert_fusion), channel_id=1, source_target_pairs={{0,2},{2,0},{4,6},{6,4},{1,3},{3,1},{5,7},{7,5},{8,10},{10,8},{12,... | collective-permute-start | bytes 196616 | tf_op jit(solution)/shard_map/ppermute | solution.py:28
  35.3 4.3 %collective-permute-start.14 = (bf16[4,64,128]{2,1,0:T(8,128)(2,1)S(1)}, bf16[4,64,128]{2,1,0:T(8,128)(2,1)S(1)}, u32[]{:S(2)}, u32[]{:S(2)}) collective-permute-start(bf16[4,64,128]{2,1,0:T(8,128)(2,1)S(1)} %add_convert_fusion), channel_id=1, source_target_pairs={{0,4},{2,6},{4,0},{6,2},{1,5},{3,7},{5,1},{7,3},{8,12},{10,14},{12... | collective-permute-start | bytes 196616 | tf_op jit(solution)/shard_map/ppermute | solution.py:28

commit v2 on v0

--- a/solution.py
+++ b/solution.py
@@ -35,8 +35,7 @@
         copy.wait()
 
 
-def pack_kernel(n_col, exciton_ref, cond_ref, after_ref, core_ref, sems):
-    del after_ref
+def pack_kernel(n_col, exciton_ref, cond_ref, core_ref, sems):
     col = lax.axis_index("col")
     copies, at = [], 0
     for source in (cond_ref, exciton_ref):
@@ -268,22 +267,29 @@
     core_rows = (cond.size + x_rows.size) // n_col // LANES
     part = n_v // n_row
     plane = lax.dynamic_slice_in_dim(orb_val[0], lax.axis_index("row") * part, part, 0)
-    planes = [swap(plane, "ka", n_ka, flip) for flip in range(1, n_ka)]
     core = pl.pallas_call(
         functools.partial(pack_kernel, n_col),
-        in_specs=[IN_HBM] * 2 + [pl.BlockSpec(memory_space=pl.ANY)],
+        in_specs=[IN_HBM] * 2,
         out_specs=IN_VMEM,
         out_shape=jax.ShapeDtypeStruct((core_rows, LANES), BF16),
         scratch_shapes=[pltpu.SemaphoreType.DMA(((n_mu + n_c) // LANES,))],
         compiler_params=pltpu.CompilerParams(vmem_limit_bytes=4 * MIB),
         name="pack",
-    )(x_rows, cond, planes[0])
+    )(x_rows, cond)
+    planes = [plane]
+    for flip in range(1, n_ka):
+        last = flip & -flip
+        source = planes[flip - last]
+        if flip > last:
+            source = after(source, core)
+        planes.append(swap(source, "ka", n_ka, last))
+    planes = planes[1:]
     joined = join(planes)
     cores = [core]
     for flip in range(1, n_ka):
         last = flip & -flip
         source = cores[flip - last]
-        if flip == last and flip > 1:
+        if flip == last:
             source = after(source, planes[flip - 1])
         cores.append(swap(source, "ka", n_ka, last))
         if flip == 2:

time: 39.9 us -> 41.6 us (1.043)
  starting transfers between devices: 16.8 us -> 22.8 us
  waiting for transfers between devices: 10.4 us -> 6.02 us
    ppermute x16, starting transfers between devices: 16.8 us -> 22.8 us  [swap(): return lax.ppermute(value, axis, [(i, i ^ flip) for i in range(size)])]
    ppermute x16, waiting for transfers between devices: 10.4 us -> 6.02 us  [swap(): return lax.ppermute(value, axis, [(i, i ^ flip) for i in range(size)])]
  transfers between devices with their start and end apart: 16 -> 16, of which waited for: 10 -> 6; matrix products, arithmetic and copies ran while one was open for 0% -> 0% of each run, Pallas kernels for 14% -> 14%
where the time goes in v2:
time: 41.6 us; the launch traced here: 41.3 us
  starting transfers between devices  22.8 us (55%)
  Pallas kernels  10.9 us (26%)
  waiting for transfers between devices  6.02 us (14%)
  local copies, waits for them, and re-layouts  0.84 us (2%)
  other arithmetic  0.71 us (2%)
    ppermute x16, starting transfers between devices, swap(): return lax.ppermute(value, axis, [(i, i ^ flip) for i in range(size)])  22.8 us
    ppermute x16, waiting for transfers between devices, swap(): return lax.ppermute(value, axis, [(i, i ^ flip) for i in range(size)])  6.02 us
    pallas_call x1, Pallas kernels, local(): pl.pallas_call(functools.partial(direct_kernel, sizes, early, factor), in...  5.25 us
    pallas_call x1, Pallas kernels, local(): pl.pallas_call(own_kernel, in_specs=[IN_SMEM] + [IN_HBM] * 4 + [pl.BlockS...  4.05 us
    pallas_call x1, Pallas kernels, local(): pl.pallas_call(functools.partial(pack_kernel, n_col), in_specs=[IN_HBM] *...  0.95 us
    dynamic_slice x1, local copies, waits for them, and re-layouts, local(): lax.dynamic_slice_in_dim(orb_val[0], lax.axis_index('row') * part, part, 0)  0.84 us
  transfers between devices with their start and end apart: 16, of which 6 were waited for; matrix products, arithmetic and copies ran while one was open for 0% of the time, Pallas kernels for 14%

profile of v2, /device:TPU:0, one launch (start us, length us, event | category | flops | bytes accessed | tf_op | source)
XLA Modules:
  0.0 41.3 jit_solution(17912304999777862010)
XLA Ops:
  0.0 0.8 %dynamic-slice_bitcast_fusion = bf16[32,1024]{1,0:T(8,128)(2,1)S(1)} fusion(bf16[1,128,1024]{2,1,0:T(8,128)(2,1)} %param.7, s32[]{:T(128)S(6)} %select_n.3), kind=kLoop, calls=%fused_computation.2 | loop fusion | bytes 131076 | tf_op jit(solution)/shard_map/dynamic_slice | solution.py:269
  0.8 4.0 %collective-permute-start = (bf16[32,1024]{1,0:T(8,128)(2,1)S(1)}, bf16[32,1024]{1,0:T(8,128)(2,1)S(1)}, u32[]{:S(2)}, u32[]{:S(2)}) collective-permute-start(bf16[32,1024]{1,0:T(8,128)(2,1)S(1)} %dynamic-slice_bitcast_fusion), channel_id=1, source_target_pairs={{0,16},{8,24},{16,0},{24,8},{1,17},{9,25},{17,1},{25,9},{2,18},{10... | collective-permute-start | bytes 196616 | tf_op jit(solution)/shard_map/ppermute | solution.py:28
  4.9 1.6 %collective-permute-start.2 = (bf16[32,1024]{1,0:T(8,128)(2,1)S(1)}, bf16[32,1024]{1,0:T(8,128)(2,1)S(1)}, u32[]{:S(2)}, u32[]{:S(2)}) collective-permute-start(bf16[32,1024]{1,0:T(8,128)(2,1)S(1)} %dynamic-slice_bitcast_fusion), channel_id=1, source_target_pairs={{0,8},{8,0},{16,24},{24,16},{1,9},{9,1},{17,25},{25,17},{2,10},{10... | collective-permute-start | bytes 196616 | tf_op jit(solution)/shard_map/ppermute | solution.py:28
  6.5 1.0 %pack.1.refs_0_.refs_1_ = bf16[512,128]{1,0:T(8,128)(2,1)S(1)} custom-call(bf16[512,128]{1,0:T(8,128)(2,1)} %bitcast.7, bf16[128,512]{1,0:T(8,128)(2,1)} %bitcast.9), custom_call_target="tpu_custom_call" | custom-call | tf_op jit(solution)/shard_map/pack/pallas_call | solution.py:270
  7.4 0.5 %collective-permute-done.refs_1_.refs_0_ = bf16[32,1024]{1,0:T(8,128)(2,1)S(1)} collective-permute-done((bf16[32,1024]{1,0:T(8,128)(2,1)S(1)}, bf16[32,1024]{1,0:T(8,128)(2,1)S(1)}, u32[]{:S(2)}, u32[]{:S(2)}) %collective-permute-start) | collective-permute-done | bytes 65568 | tf_op jit(solution)/shard_map/ppermute | solution.py:28
  7.9 1.4 %collective-permute-start.3 = (bf16[32,1024]{1,0:T(8,128)(2,1)S(1)}, bf16[32,1024]{1,0:T(8,128)(2,1)S(1)}, u32[]{:S(2)}, u32[]{:S(2)}) collective-permute-start(bf16[32,1024]{1,0:T(8,128)(2,1)S(1)} %after.6), channel_id=1, source_target_pairs={{0,8},{8,0},{16,24},{24,16},{1,9},{9,1},{17,25},{25,17},{2,10},{10... | collective-permute-start | bytes 196616 | tf_op jit(solution)/shard_map/ppermute | solution.py:28
  9.3 0.0 collective-permute-done.2.refs_0_.refs_1_
  9.3 1.5 %collective-permute-start.4 = (bf16[512,128]{1,0:T(8,128)(2,1)S(1)}, bf16[512,128]{1,0:T(8,128)(2,1)S(1)}, u32[]{:S(2)}, u32[]{:S(2)}) collective-permute-start(bf16[512,128]{1,0:T(8,128)(2,1)S(1)} %after.7), channel_id=1, source_target_pairs={{0,8},{8,0},{16,24},{24,16},{1,9},{9,1},{17,25},{25,17},{2,10},{10... | collective-permute-start | bytes 393224 | tf_op jit(solution)/shard_map/ppermute | solution.py:28
  10.8 2.0 %collective-permute-start.1 = (bf16[512,128]{1,0:T(8,128)(2,1)S(1)}, bf16[512,128]{1,0:T(8,128)(2,1)S(1)}, u32[]{:S(2)}, u32[]{:S(2)}) collective-permute-start(bf16[512,128]{1,0:T(8,128)(2,1)S(1)} %after.5), channel_id=1, source_target_pairs={{0,16},{8,24},{16,0},{24,8},{1,17},{9,25},{17,1},{25,9},{2,18},{10... | collective-permute-start | bytes 393224 | tf_op jit(solution)/shard_map/ppermute | solution.py:28
  12.8 0.0 collective-permute-done.3.refs_2_
  12.8 4.3 %collective-permute-start.11 = (bf16[96,1024]{1,0:T(8,128)(2,1)S(1)}, bf16[96,1024]{1,0:T(8,128)(2,1)S(1)}, u32[]{:S(2)}, u32[]{:S(2)}) collective-permute-start(bf16[96,1024]{1,0:T(8,128)(2,1)S(1)} %join.1.refs_1_.refs_0_), channel_id=1, source_target_pairs={{0,6},{2,4},{4,2},{6,0},{1,7},{3,5},{5,3},{7,1},{8,14},{10,12},{12... | collective-permute-start | bytes 589832 | tf_op jit(solution)/shard_map/ppermute | solution.py:28
  17.1 0.5 %collective-permute-start.10 = (bf16[96,1024]{1,0:T(8,128)(2,1)S(1)}, bf16[96,1024]{1,0:T(8,128)(2,1)S(1)}, u32[]{:S(2)}, u32[]{:S(2)}) collective-permute-start(bf16[96,1024]{1,0:T(8,128)(2,1)S(1)} %join.1.refs_1_.refs_0_), channel_id=1, source_target_pairs={{0,4},{2,6},{4,0},{6,2},{1,5},{3,7},{5,1},{7,3},{8,12},{10,14},{12... | collective-permute-start | bytes 589832 | tf_op jit(solution)/shard_map/ppermute | solution.py:28
  17.6 0.1 collective-permute-start.9
  17.8 0.0 collective-permute-done.4.refs_2_.refs_0_
  17.8 0.0 collective-permute-done.1.refs_0_
  17.8 2.8 %collective-permute-start.7 = (bf16[512,128]{1,0:T(8,128)(2,1)S(1)}, bf16[512,128]{1,0:T(8,128)(2,1)S(1)}, u32[]{:S(2)}, u32[]{:S(2)}) collective-permute-start(bf16[512,128]{1,0:T(8,128)(2,1)S(1)} %after.8.after_ref.refs_2_), channel_id=1, source_target_pairs={{0,8},{8,0},{16,24},{24,16},{1,9},{9,1},{17,25},{25,17},{2,10},{10... | collective-permute-start | bytes 393224 | tf_op jit(solution)/shard_map/ppermute | solution.py:28
  20.6 0.0 collective-permute-start.6
  20.6 4.0 %own_term.1 = (f32[4,512,1024]{2,1,0:T(8,128)S(1)}, bf16[3,512,1024]{2,1,0:T(8,128)(2,1)S(1)}, bf16[128,512]{1,0:T(8,128)(2,1)S(1)}, bf16[128,1024]{1,0:T(8,128)(2,1)S(1)}) custom-call(s32[4,4]{1,0:T(4,128)} %q_ref.1, bf16[4,512,1024]{2,1,0:T(8,128)(2,1)} %w_ref.1, bf16[512,128]{1,0:T(8,128)(2,1)} %bitcast.8, bf16[128,512]{1,0:T(8,128)(2,1)} %bitcast.10, ...), custom_call_target="tpu_custom_call" | custom-call | bytes 8388608 | tf_op jit(solution)/shard_map/own_term/pallas_call | solution.py:298
  24.6 0.0 collective-permute-done.7.refs_5_
  24.6 0.6 %collective-permute-start.5 = (bf16[512,128]{1,0:T(8,128)(2,1)S(1)}, bf16[512,128]{1,0:T(8,128)(2,1)S(1)}, u32[]{:S(2)}, u32[]{:S(2)}) collective-permute-start(bf16[512,128]{1,0:T(8,128)(2,1)S(1)} %collective-permute-done.4.refs_2_.refs_0_), channel_id=1, source_target_pairs={{0,1},{1,0},{2,3},{3,2},{4,5},{5,4},{6,7},{7,6},{8,9},{9,8},{10,11... | collective-permute-start | bytes 393224 | tf_op jit(solution)/shard_map/ppermute | solution.py:28
  25.2 0.0 collective-permute-done.11.refs_3_
  25.2 0.1 collective-permute-start.8
  25.3 0.0 collective-permute-done.10.refs_2_
  25.3 0.0 collective-permute-done.9.refs_1_
  25.3 0.1 spread.1.refs_7_
  25.4 0.8 %collective-permute-done.5.refs_1_ = bf16[512,128]{1,0:T(8,128)(2,1)S(1)} collective-permute-done((bf16[512,128]{1,0:T(8,128)(2,1)S(1)}, bf16[512,128]{1,0:T(8,128)(2,1)S(1)}, u32[]{:S(2)}, u32[]{:S(2)}) %collective-permute-start.5) | collective-permute-done | bytes 131104 | tf_op jit(solution)/shard_map/ppermute | solution.py:28
  26.2 0.0 collective-permute-done.6.refs_3_
  26.2 0.5 %panels.1.refs_4_ = bf16[2,4,512,128]{3,2,1,0:T(8,128)(2,1)S(1)} custom-call(bf16[512,128]{1,0:T(8,128)(2,1)S(1)} %collective-permute-done.4.refs_2_.refs_0_, bf16[512,128]{1,0:T(8,128)(2,1)S(1)} %collective-permute-done.5.refs_1_, bf16[512,128]{1,0:T(8,128)(2,1)S(1)} %after.8.after_ref.refs_2_, bf16[512,128]{1,0:T(8,128)(2,1)S(1)} %collective-permute-done.6.refs_3_), custom_call_target="tpu_custom_call" | custom-call | flops 1000000000 | tf_op jit(solution)/shard_map/panels/pallas_call | solution.py:325
  26.7 0.0 collective-permute-done.8.refs_6_
  26.7 5.3 %direct_term.1 = (f32[4,64,128]{2,1,0:T(8,128)S(1)}, bf16[4,64,128]{2,1,0:T(8,128)(2,1)S(1)}) custom-call(f32[4,512,1024]{2,1,0:T(8,128)S(1)} %get-tuple-element.11.refs_0_, bf16[3,512,1024]{2,1,0:T(8,128)(2,1)S(1)} %get-tuple-element.12.refs_1_, bf16[128,512]{1,0:T(8,128)(2,1)S(1)} %get-tuple-element.13.refs_2_, ...), custom_call_target="tpu_custom_call" | custom-call | tf_op jit(solution)/shard_map/direct_term/pallas_call | solution.py:353
  32.0 0.4 %collective-permute-start.12 = (bf16[4,64,128]{2,1,0:T(8,128)(2,1)S(1)}, bf16[4,64,128]{2,1,0:T(8,128)(2,1)S(1)}, u32[]{:S(2)}, u32[]{:S(2)}) collective-permute-start(bf16[4,64,128]{2,1,0:T(8,128)(2,1)S(1)} %get-tuple-element.16), channel_id=1, source_target_pairs={{0,1},{1,0},{2,3},{3,2},{4,5},{5,4},{6,7},{7,6},{8,9},{9,8},{10,11... | collective-permute-start | bytes 196616 | tf_op jit(solution)/shard_map/ppermute | solution.py:28
  32.4 0.9 %collective-permute-done.12 = bf16[4,64,128]{2,1,0:T(8,128)(2,1)S(1)} collective-permute-done((bf16[4,64,128]{2,1,0:T(8,128)(2,1)S(1)}, bf16[4,64,128]{2,1,0:T(8,128)(2,1)S(1)}, u32[]{:S(2)}, u32[]{:S(2)}) %collective-permute-start.12) | collective-permute-done | bytes 65568 | tf_op jit(solution)/shard_map/ppermute | solution.py:28
  33.3 2.5 %collective-permute-start.13 = (bf16[4,64,128]{2,1,0:T(8,128)(2,1)S(1)}, bf16[4,64,128]{2,1,0:T(8,128)(2,1)S(1)}, u32[]{:S(2)}, u32[]{:S(2)}) collective-permute-start(bf16[4,64,128]{2,1,0:T(8,128)(2,1)S(1)} %add_convert_fusion), channel_id=1, source_target_pairs={{0,6},{2,4},{4,2},{6,0},{1,7},{3,5},{5,3},{7,1},{8,14},{10,12},{12... | collective-permute-start | bytes 196616 | tf_op jit(solution)/shard_map/ppermute | solution.py:28
  35.8 0.5 %collective-permute-start.15 = (bf16[4,64,128]{2,1,0:T(8,128)(2,1)S(1)}, bf16[4,64,128]{2,1,0:T(8,128)(2,1)S(1)}, u32[]{:S(2)}, u32[]{:S(2)}) collective-permute-start(bf16[4,64,128]{2,1,0:T(8,128)(2,1)S(1)} %add_convert_fusion), channel_id=1, source_target_pairs={{0,2},{2,0},{4,6},{6,4},{1,3},{3,1},{5,7},{7,5},{8,10},{10,8},{12,... | collective-permute-start | bytes 196616 | tf_op jit(solution)/shard_map/ppermute | solution.py:28
  36.4 0.5 %collective-permute-start.14 = (bf16[4,64,128]{2,1,0:T(8,128)(2,1)S(1)}, bf16[4,64,128]{2,1,0:T(8,128)(2,1)S(1)}, u32[]{:S(2)}, u32[]{:S(2)}) collective-permute-start(bf16[4,64,128]{2,1,0:T(8,128)(2,1)S(1)} %add_convert_fusion), channel_id=1, source_target_pairs={{0,4},{2,6},{4,0},{6,2},{1,5},{3,7},{5,1},{7,3},{8,12},{10,14},{12... | collective-permute-start | bytes 196616 | tf_op jit(solution)/shard_map/ppermute | solution.py:28
  36.9 2.0 %collective-permute-done.13.refs_0_ = bf16[4,64,128]{2,1,0:T(8,128)(2,1)S(1)} collective-permute-done((bf16[4,64,128]{2,1,0:T(8,128)(2,1)S(1)}, bf16[4,64,128]{2,1,0:T(8,128)(2,1)S(1)}, u32[]{:S(2)}, u32[]{:S(2)}) %collective-permute-start.13) | collective-permute-done | bytes 65568 | tf_op jit(solution)/shard_map/ppermute | solution.py:28
  38.9 1.2 %collective-permute-done.15 = bf16[4,64,128]{2,1,0:T(8,128)(2,1)S(1)} collective-permute-done((bf16[4,64,128]{2,1,0:T(8,128)(2,1)S(1)}, bf16[4,64,128]{2,1,0:T(8,128)(2,1)S(1)}, u32[]{:S(2)}, u32[]{:S(2)}) %collective-permute-start.15) | collective-permute-done | bytes 65568 | tf_op jit(solution)/shard_map/ppermute | solution.py:28
  40.1 0.5 %collective-permute-done.14 = bf16[4,64,128]{2,1,0:T(8,128)(2,1)S(1)} collective-permute-done((bf16[4,64,128]{2,1,0:T(8,128)(2,1)S(1)}, bf16[4,64,128]{2,1,0:T(8,128)(2,1)S(1)}, u32[]{:S(2)}, u32[]{:S(2)}) %collective-permute-start.14) | collective-permute-done | bytes 65568 | tf_op jit(solution)/shard_map/ppermute | solution.py:28
  40.6 0.7 %add_bitcast_fusion = f32[1,4,64,128]{3,2,1,0:T(8,128)} fusion(bf16[4,64,128]{2,1,0:T(8,128)(2,1)S(1)} %add_convert_fusion, bf16[4,64,128]{2,1,0:T(8,128)(2,1)S(1)} %collective-permute-done.15, bf16[4,64,128]{2,1,0:T(8,128)(2,1)S(1)} %collective-permute-done.14, bf16[4,64,128]{2,1,0:T(8,128)(2,1)S(1)} %after.9), kind=kLoop, calls=%fused_computation | loop fusion | flops 229376 | bytes 393216 | tf_op jit(solution)/shard_map/broadcast_in_dim | solution.py:381
  (7 shorter events, 0.1 us)
Async XLA Ops:
  0.8 7.1 %collective-permute-start = (bf16[32,1024]{1,0:T(8,128)(2,1)S(1)}, bf16[32,1024]{1,0:T(8,128)(2,1)S(1)}, u32[]{:S(2)}, u32[]{:S(2)}) collective-permute-start(bf16[32,1024]{1,0:T(8,128)(2,1)S(1)} %dynamic-slice_bitcast_fusion), channel_id=1, source_target_pairs={{0,16},{8,24},{16,0},{24,8},{1,17},{9,25},{17,1},{25,9},{2,18},{10... | collective-permute-start | bytes 196616 | tf_op jit(solution)/shard_map/ppermute | solution.py:28
  4.9 4.4 %collective-permute-start.2 = (bf16[32,1024]{1,0:T(8,128)(2,1)S(1)}, bf16[32,1024]{1,0:T(8,128)(2,1)S(1)}, u32[]{:S(2)}, u32[]{:S(2)}) collective-permute-start(bf16[32,1024]{1,0:T(8,128)(2,1)S(1)} %dynamic-slice_bitcast_fusion), channel_id=1, source_target_pairs={{0,8},{8,0},{16,24},{24,16},{1,9},{9,1},{17,25},{25,17},{2,10},{10... | collective-permute-start | bytes 196616 | tf_op jit(solution)/shard_map/ppermute | solution.py:28
  7.9 4.8 %collective-permute-start.3 = (bf16[32,1024]{1,0:T(8,128)(2,1)S(1)}, bf16[32,1024]{1,0:T(8,128)(2,1)S(1)}, u32[]{:S(2)}, u32[]{:S(2)}) collective-permute-start(bf16[32,1024]{1,0:T(8,128)(2,1)S(1)} %after.6), channel_id=1, source_target_pairs={{0,8},{8,0},{16,24},{24,16},{1,9},{9,1},{17,25},{25,17},{2,10},{10... | collective-permute-start | bytes 196616 | tf_op jit(solution)/shard_map/ppermute | solution.py:28
  9.3 8.4 %collective-permute-start.4 = (bf16[512,128]{1,0:T(8,128)(2,1)S(1)}, bf16[512,128]{1,0:T(8,128)(2,1)S(1)}, u32[]{:S(2)}, u32[]{:S(2)}) collective-permute-start(bf16[512,128]{1,0:T(8,128)(2,1)S(1)} %after.7), channel_id=1, source_target_pairs={{0,8},{8,0},{16,24},{24,16},{1,9},{9,1},{17,25},{25,17},{2,10},{10... | collective-permute-start | bytes 393224 | tf_op jit(solution)/shard_map/ppermute | solution.py:28
  10.8 7.0 %collective-permute-start.1 = (bf16[512,128]{1,0:T(8,128)(2,1)S(1)}, bf16[512,128]{1,0:T(8,128)(2,1)S(1)}, u32[]{:S(2)}, u32[]{:S(2)}) collective-permute-start(bf16[512,128]{1,0:T(8,128)(2,1)S(1)} %after.5), channel_id=1, source_target_pairs={{0,16},{8,24},{16,0},{24,8},{1,17},{9,25},{17,1},{25,9},{2,18},{10... | collective-permute-start | bytes 393224 | tf_op jit(solution)/shard_map/ppermute | solution.py:28
  12.8 12.4 %collective-permute-start.11 = (bf16[96,1024]{1,0:T(8,128)(2,1)S(1)}, bf16[96,1024]{1,0:T(8,128)(2,1)S(1)}, u32[]{:S(2)}, u32[]{:S(2)}) collective-permute-start(bf16[96,1024]{1,0:T(8,128)(2,1)S(1)} %join.1.refs_1_.refs_0_), channel_id=1, source_target_pairs={{0,6},{2,4},{4,2},{6,0},{1,7},{3,5},{5,3},{7,1},{8,14},{10,12},{12... | collective-permute-start | bytes 589832 | tf_op jit(solution)/shard_map/ppermute | solution.py:28
  17.1 8.2 %collective-permute-start.10 = (bf16[96,1024]{1,0:T(8,128)(2,1)S(1)}, bf16[96,1024]{1,0:T(8,128)(2,1)S(1)}, u32[]{:S(2)}, u32[]{:S(2)}) collective-permute-start(bf16[96,1024]{1,0:T(8,128)(2,1)S(1)} %join.1.refs_1_.refs_0_), channel_id=1, source_target_pairs={{0,4},{2,6},{4,0},{6,2},{1,5},{3,7},{5,1},{7,3},{8,12},{10,14},{12... | collective-permute-start | bytes 589832 | tf_op jit(solution)/shard_map/ppermute | solution.py:28
  17.6 7.7 %collective-permute-start.9 = (bf16[96,1024]{1,0:T(8,128)(2,1)S(1)}, bf16[96,1024]{1,0:T(8,128)(2,1)S(1)}, u32[]{:S(2)}, u32[]{:S(2)}) collective-permute-start(bf16[96,1024]{1,0:T(8,128)(2,1)S(1)} %join.1.refs_1_.refs_0_), channel_id=1, source_target_pairs={{0,2},{2,0},{4,6},{6,4},{1,3},{3,1},{5,7},{7,5},{8,10},{10,8},{12,... | collective-permute-start | bytes 589832 | tf_op jit(solution)/shard_map/ppermute | solution.py:28
  17.8 6.8 %collective-permute-start.7 = (bf16[512,128]{1,0:T(8,128)(2,1)S(1)}, bf16[512,128]{1,0:T(8,128)(2,1)S(1)}, u32[]{:S(2)}, u32[]{:S(2)}) collective-permute-start(bf16[512,128]{1,0:T(8,128)(2,1)S(1)} %after.8.after_ref.refs_2_), channel_id=1, source_target_pairs={{0,8},{8,0},{16,24},{24,16},{1,9},{9,1},{17,25},{25,17},{2,10},{10... | collective-permute-start | bytes 393224 | tf_op jit(solution)/shard_map/ppermute | solution.py:28
  20.6 5.6 %collective-permute-start.6 = (bf16[512,128]{1,0:T(8,128)(2,1)S(1)}, bf16[512,128]{1,0:T(8,128)(2,1)S(1)}, u32[]{:S(2)}, u32[]{:S(2)}) collective-permute-start(bf16[512,128]{1,0:T(8,128)(2,1)S(1)} %after.8.after_ref.refs_2_), channel_id=1, source_target_pairs={{0,1},{1,0},{2,3},{3,2},{4,5},{5,4},{6,7},{7,6},{8,9},{9,8},{10,11... | collective-permute-start | bytes 393224 | tf_op jit(solution)/shard_map/ppermute | solution.py:28
  24.6 1.6 %collective-permute-start.5 = (bf16[512,128]{1,0:T(8,128)(2,1)S(1)}, bf16[512,128]{1,0:T(8,128)(2,1)S(1)}, u32[]{:S(2)}, u32[]{:S(2)}) collective-permute-start(bf16[512,128]{1,0:T(8,128)(2,1)S(1)} %collective-permute-done.4.refs_2_.refs_0_), channel_id=1, source_target_pairs={{0,1},{1,0},{2,3},{3,2},{4,5},{5,4},{6,7},{7,6},{8,9},{9,8},{10,11... | collective-permute-start | bytes 393224 | tf_op jit(solution)/shard_map/ppermute | solution.py:28
  25.2 1.5 %collective-permute-start.8 = (bf16[512,128]{1,0:T(8,128)(2,1)S(1)}, bf16[512,128]{1,0:T(8,128)(2,1)S(1)}, u32[]{:S(2)}, u32[]{:S(2)}) collective-permute-start(bf16[512,128]{1,0:T(8,128)(2,1)S(1)} %collective-permute-done.7.refs_5_), channel_id=1, source_target_pairs={{0,1},{1,0},{2,3},{3,2},{4,5},{5,4},{6,7},{7,6},{8,9},{9,8},{10,11... | collective-permute-start | bytes 393224 | tf_op jit(solution)/shard_map/ppermute | solution.py:28
  32.0 1.3 %collective-permute-start.12 = (bf16[4,64,128]{2,1,0:T(8,128)(2,1)S(1)}, bf16[4,64,128]{2,1,0:T(8,128)(2,1)S(1)}, u32[]{:S(2)}, u32[]{:S(2)}) collective-permute-start(bf16[4,64,128]{2,1,0:T(8,128)(2,1)S(1)} %get-tuple-element.16), channel_id=1, source_target_pairs={{0,1},{1,0},{2,3},{3,2},{4,5},{5,4},{6,7},{7,6},{8,9},{9,8},{10,11... | collective-permute-start | bytes 196616 | tf_op jit(solution)/shard_map/ppermute | solution.py:28
  33.3 5.6 %collective-permute-start.13 = (bf16[4,64,128]{2,1,0:T(8,128)(2,1)S(1)}, bf16[4,64,128]{2,1,0:T(8,128)(2,1)S(1)}, u32[]{:S(2)}, u32[]{:S(2)}) collective-permute-start(bf16[4,64,128]{2,1,0:T(8,128)(2,1)S(1)} %add_convert_fusion), channel_id=1, source_target_pairs={{0,6},{2,4},{4,2},{6,0},{1,7},{3,5},{5,3},{7,1},{8,14},{10,12},{12... | collective-permute-start | bytes 196616 | tf_op jit(solution)/shard_map/ppermute | solution.py:28
  35.8 4.3 %collective-permute-start.15 = (bf16[4,64,128]{2,1,0:T(8,128)(2,1)S(1)}, bf16[4,64,128]{2,1,0:T(8,128)(2,1)S(1)}, u32[]{:S(2)}, u32[]{:S(2)}) collective-permute-start(bf16[4,64,128]{2,1,0:T(8,128)(2,1)S(1)} %add_convert_fusion), channel_id=1, source_target_pairs={{0,2},{2,0},{4,6},{6,4},{1,3},{3,1},{5,7},{7,5},{8,10},{10,8},{12,... | collective-permute-start | bytes 196616 | tf_op jit(solution)/shard_map/ppermute | solution.py:28
  36.4 4.3 %collective-permute-start.14 = (bf16[4,64,128]{2,1,0:T(8,128)(2,1)S(1)}, bf16[4,64,128]{2,1,0:T(8,128)(2,1)S(1)}, u32[]{:S(2)}, u32[]{:S(2)}) collective-permute-start(bf16[4,64,128]{2,1,0:T(8,128)(2,1)S(1)} %add_convert_fusion), channel_id=1, source_target_pairs={{0,4},{2,6},{4,0},{6,2},{1,5},{3,7},{5,1},{7,3},{8,12},{10,14},{12... | collective-permute-start | bytes 196616 | tf_op jit(solution)/shard_map/ppermute | solution.py:28

commit v3 on v0

--- a/solution.py
+++ b/solution.py
@@ -12,7 +12,7 @@
 F32 = jnp.float32
 LANES = 128
 ROWS = 16
-TILE = 128
+TILE = 64
 CHUNK = 256
 QUARTERS = 4
 MIB = 2**20

time: 39.9 us -> 41.1 us (1.030)
  Pallas kernels: 10.9 us -> 12.2 us
    pallas_call x1, Pallas kernels: 4.06 us -> 4.61 us  [local(): pl.pallas_call(own_kernel, in_specs=[IN_SMEM] + [IN_HBM] * 4 + [pl.BlockS...]
    pallas_call x1, Pallas kernels: 0.49 us -> 1.03 us  [local(): pl.pallas_call(functools.partial(panels_kernel, n_col, n_v), in_specs=[IN...]
  transfers between devices with their start and end apart: 16 -> 16, of which waited for: 10 -> 8; matrix products, arithmetic and copies ran while one was open for 0% -> 0% of each run, Pallas kernels for 14% -> 16%
where the time goes in v3:
time: 41.1 us; the launch traced here: 40.9 us
  starting transfers between devices  17 us (41%)
  Pallas kernels  12.2 us (30%)
  waiting for transfers between devices  10.1 us (25%)
  local copies, waits for them, and re-layouts  0.84 us (2%)
  other arithmetic  0.71 us (2%)
    ppermute x16, starting transfers between devices, swap(): return lax.ppermute(value, axis, [(i, i ^ flip) for i in range(size)])  17 us
    ppermute x16, waiting for transfers between devices, swap(): return lax.ppermute(value, axis, [(i, i ^ flip) for i in range(size)])  10.1 us
    pallas_call x1, Pallas kernels, local(): pl.pallas_call(functools.partial(direct_kernel, sizes, early, factor), in...  5.48 us
    pallas_call x1, Pallas kernels, local(): pl.pallas_call(own_kernel, in_specs=[IN_SMEM] + [IN_HBM] * 4 + [pl.BlockS...  4.61 us
    pallas_call x1, Pallas kernels, local(): pl.pallas_call(functools.partial(panels_kernel, n_col, n_v), in_specs=[IN...  1.03 us
    pallas_call x1, Pallas kernels, local(): pl.pallas_call(functools.partial(pack_kernel, n_col), in_specs=[IN_HBM] *...  0.95 us
    dynamic_slice x1, local copies, waits for them, and re-layouts, local(): lax.dynamic_slice_in_dim(orb_val[0], lax.axis_index('row') * part, part, 0)  0.84 us
  transfers between devices with their start and end apart: 16, of which 8 were waited for; matrix products, arithmetic and copies ran while one was open for 0% of the time, Pallas kernels for 16%

profile of v3, /device:TPU:0, one launch (start us, length us, event | category | flops | bytes accessed | tf_op | source)
XLA Modules:
  0.0 40.9 jit_solution(860054466570132230)
XLA Ops:
  0.0 0.8 %dynamic-slice_bitcast_fusion = bf16[32,1024]{1,0:T(8,128)(2,1)S(1)} fusion(bf16[1,128,1024]{2,1,0:T(8,128)(2,1)} %param.7, s32[]{:T(128)S(6)} %select_n.3), kind=kLoop, calls=%fused_computation.2 | loop fusion | bytes 131076 | tf_op jit(solution)/shard_map/dynamic_slice | solution.py:270
  0.8 3.0 %collective-permute-start = (bf16[32,1024]{1,0:T(8,128)(2,1)S(1)}, bf16[32,1024]{1,0:T(8,128)(2,1)S(1)}, u32[]{:S(2)}, u32[]{:S(2)}) collective-permute-start(bf16[32,1024]{1,0:T(8,128)(2,1)S(1)} %dynamic-slice_bitcast_fusion), channel_id=1, source_target_pairs={{0,8},{8,0},{16,24},{24,16},{1,9},{9,1},{17,25},{25,17},{2,10},{10... | collective-permute-start | bytes 196616 | tf_op jit(solution)/shard_map/ppermute | solution.py:28
  3.9 2.6 %collective-permute-start.1 = (bf16[32,1024]{1,0:T(8,128)(2,1)S(1)}, bf16[32,1024]{1,0:T(8,128)(2,1)S(1)}, u32[]{:S(2)}, u32[]{:S(2)}) collective-permute-start(bf16[32,1024]{1,0:T(8,128)(2,1)S(1)} %dynamic-slice_bitcast_fusion), channel_id=1, source_target_pairs={{0,16},{8,24},{16,0},{24,8},{1,17},{9,25},{17,1},{25,9},{2,18},{10... | collective-permute-start | bytes 196616 | tf_op jit(solution)/shard_map/ppermute | solution.py:28
  6.5 0.0 collective-permute-start.3
  6.5 0.0 collective-permute-done.after_ref.refs_0_
  6.5 1.0 %pack.1.refs_0_ = bf16[512,128]{1,0:T(8,128)(2,1)S(1)} custom-call(bf16[512,128]{1,0:T(8,128)(2,1)} %bitcast.7, bf16[128,512]{1,0:T(8,128)(2,1)} %bitcast.9, bf16[32,1024]{1,0:T(8,128)(2,1)S(1)} %collective-permute-done.after_ref.refs_0_), custom_call_target="tpu_custom_call" | custom-call | tf_op jit(solution)/shard_map/pack/pallas_call | solution.py:272
  7.4 1.7 %collective-permute-start.4 = (bf16[512,128]{1,0:T(8,128)(2,1)S(1)}, bf16[512,128]{1,0:T(8,128)(2,1)S(1)}, u32[]{:S(2)}, u32[]{:S(2)}) collective-permute-start(bf16[512,128]{1,0:T(8,128)(2,1)S(1)} %pack.1.refs_0_), channel_id=1, source_target_pairs={{0,8},{8,0},{16,24},{24,16},{1,9},{9,1},{17,25},{25,17},{2,10},{10... | collective-permute-start | bytes 393224 | tf_op jit(solution)/shard_map/ppermute | solution.py:28
  9.2 2.0 %collective-permute-done.1.refs_1_ = bf16[32,1024]{1,0:T(8,128)(2,1)S(1)} collective-permute-done((bf16[32,1024]{1,0:T(8,128)(2,1)S(1)}, bf16[32,1024]{1,0:T(8,128)(2,1)S(1)}, u32[]{:S(2)}, u32[]{:S(2)}) %collective-permute-start.1) | collective-permute-done | bytes 65568 | tf_op jit(solution)/shard_map/ppermute | solution.py:28
  11.2 1.3 %collective-permute-start.2 = (bf16[512,128]{1,0:T(8,128)(2,1)S(1)}, bf16[512,128]{1,0:T(8,128)(2,1)S(1)}, u32[]{:S(2)}, u32[]{:S(2)}) collective-permute-start(bf16[512,128]{1,0:T(8,128)(2,1)S(1)} %after.3), channel_id=1, source_target_pairs={{0,16},{8,24},{16,0},{24,8},{1,17},{9,25},{17,1},{25,9},{2,18},{10... | collective-permute-start | bytes 393224 | tf_op jit(solution)/shard_map/ppermute | solution.py:28
  12.5 0.8 %collective-permute-done.3.refs_2_ = bf16[32,1024]{1,0:T(8,128)(2,1)S(1)} collective-permute-done((bf16[32,1024]{1,0:T(8,128)(2,1)S(1)}, bf16[32,1024]{1,0:T(8,128)(2,1)S(1)}, u32[]{:S(2)}, u32[]{:S(2)}) %collective-permute-start.3) | collective-permute-done | bytes 65568 | tf_op jit(solution)/shard_map/ppermute | solution.py:28
  13.2 2.5 %collective-permute-start.11 = (bf16[96,1024]{1,0:T(8,128)(2,1)S(1)}, bf16[96,1024]{1,0:T(8,128)(2,1)S(1)}, u32[]{:S(2)}, u32[]{:S(2)}) collective-permute-start(bf16[96,1024]{1,0:T(8,128)(2,1)S(1)} %join.1.refs_1_.refs_0_), channel_id=1, source_target_pairs={{0,6},{2,4},{4,2},{6,0},{1,7},{3,5},{5,3},{7,1},{8,14},{10,12},{12... | collective-permute-start | bytes 589832 | tf_op jit(solution)/shard_map/ppermute | solution.py:28
  15.8 0.5 %collective-permute-start.10 = (bf16[96,1024]{1,0:T(8,128)(2,1)S(1)}, bf16[96,1024]{1,0:T(8,128)(2,1)S(1)}, u32[]{:S(2)}, u32[]{:S(2)}) collective-permute-start(bf16[96,1024]{1,0:T(8,128)(2,1)S(1)} %join.1.refs_1_.refs_0_), channel_id=1, source_target_pairs={{0,4},{2,6},{4,0},{6,2},{1,5},{3,7},{5,1},{7,3},{8,12},{10,14},{12... | collective-permute-start | bytes 589832 | tf_op jit(solution)/shard_map/ppermute | solution.py:28
  16.3 0.5 %collective-permute-start.9 = (bf16[96,1024]{1,0:T(8,128)(2,1)S(1)}, bf16[96,1024]{1,0:T(8,128)(2,1)S(1)}, u32[]{:S(2)}, u32[]{:S(2)}) collective-permute-start(bf16[96,1024]{1,0:T(8,128)(2,1)S(1)} %join.1.refs_1_.refs_0_), channel_id=1, source_target_pairs={{0,2},{2,0},{4,6},{6,4},{1,3},{3,1},{5,7},{7,5},{8,10},{10,8},{12,... | collective-permute-start | bytes 589832 | tf_op jit(solution)/shard_map/ppermute | solution.py:28
  16.8 1.9 %collective-permute-done.2.refs_0_ = bf16[512,128]{1,0:T(8,128)(2,1)S(1)} collective-permute-done((bf16[512,128]{1,0:T(8,128)(2,1)S(1)}, bf16[512,128]{1,0:T(8,128)(2,1)S(1)}, u32[]{:S(2)}, u32[]{:S(2)}) %collective-permute-start.2) | collective-permute-done | bytes 131104 | tf_op jit(solution)/shard_map/ppermute | solution.py:28
  18.7 0.0 collective-permute-done.4.refs_2_.refs_0_
  18.7 0.1 collective-permute-start.7
  18.8 0.1 collective-permute-start.6
  18.9 4.6 %own_term.1 = (f32[8,256,1024]{2,1,0:T(8,128)S(1)}, bf16[3,512,1024]{2,1,0:T(8,128)(2,1)S(1)}, bf16[128,512]{1,0:T(8,128)(2,1)S(1)}, bf16[128,1024]{1,0:T(8,128)(2,1)S(1)}) custom-call(s32[4,4]{1,0:T(4,128)} %q_ref.1, bf16[4,512,1024]{2,1,0:T(8,128)(2,1)} %w_ref.1, bf16[512,128]{1,0:T(8,128)(2,1)} %bitcast.8, bf16[128,512]{1,0:T(8,128)(2,1)} %bitcast.10, ...), custom_call_target="tpu_custom_call" | custom-call | bytes 8388608 | tf_op jit(solution)/shard_map/own_term/pallas_call | solution.py:292
  23.5 0.0 collective-permute-done.11.refs_3_
  23.5 0.5 %collective-permute-start.5 = (bf16[512,128]{1,0:T(8,128)(2,1)S(1)}, bf16[512,128]{1,0:T(8,128)(2,1)S(1)}, u32[]{:S(2)}, u32[]{:S(2)}) collective-permute-start(bf16[512,128]{1,0:T(8,128)(2,1)S(1)} %collective-permute-done.4.refs_2_.refs_0_), channel_id=1, source_target_pairs={{0,1},{1,0},{2,3},{3,2},{4,5},{5,4},{6,7},{7,6},{8,9},{9,8},{10,11... | collective-permute-start | bytes 393224 | tf_op jit(solution)/shard_map/ppermute | solution.py:28
  24.0 0.0 collective-permute-done.7.refs_5_
  24.0 0.1 collective-permute-start.8
  24.1 0.0 collective-permute-done.10.refs_2_
  24.1 0.0 collective-permute-done.9.refs_1_
  24.1 0.1 spread.1.refs_7_
  24.2 0.0 collective-permute-done.6.refs_3_
  24.2 0.8 %collective-permute-done.5.refs_1_ = bf16[512,128]{1,0:T(8,128)(2,1)S(1)} collective-permute-done((bf16[512,128]{1,0:T(8,128)(2,1)S(1)}, bf16[512,128]{1,0:T(8,128)(2,1)S(1)}, u32[]{:S(2)}, u32[]{:S(2)}) %collective-permute-start.5) | collective-permute-done | bytes 131104 | tf_op jit(solution)/shard_map/ppermute | solution.py:28
  25.0 1.0 %panels.1.refs_4_ = bf16[2,8,256,128]{3,2,1,0:T(8,128)(2,1)S(1)} custom-call(bf16[512,128]{1,0:T(8,128)(2,1)S(1)} %collective-permute-done.4.refs_2_.refs_0_, bf16[512,128]{1,0:T(8,128)(2,1)S(1)} %collective-permute-done.5.refs_1_, bf16[512,128]{1,0:T(8,128)(2,1)S(1)} %after.4.after_ref.refs_2_, bf16[512,128]{1,0:T(8,128)(2,1)S(1)} %collective-permute-done.6.refs_3_), custom_call_target="tpu_custom_call" | custom-call | flops 1000000000 | tf_op jit(solution)/shard_map/panels/pallas_call | solution.py:319
  26.1 0.0 collective-permute-done.8.refs_6_
  26.1 5.5 %direct_term.1 = (f32[4,64,128]{2,1,0:T(8,128)S(1)}, bf16[4,64,128]{2,1,0:T(8,128)(2,1)S(1)}) custom-call(f32[8,256,1024]{2,1,0:T(8,128)S(1)} %get-tuple-element.11.refs_0_, bf16[3,512,1024]{2,1,0:T(8,128)(2,1)S(1)} %get-tuple-element.12.refs_1_, bf16[128,512]{1,0:T(8,128)(2,1)S(1)} %get-tuple-element.13.refs_2_, ...), custom_call_target="tpu_custom_call" | custom-call | tf_op jit(solution)/shard_map/direct_term/pallas_call | solution.py:347
  31.6 0.4 %collective-permute-start.12 = (bf16[4,64,128]{2,1,0:T(8,128)(2,1)S(1)}, bf16[4,64,128]{2,1,0:T(8,128)(2,1)S(1)}, u32[]{:S(2)}, u32[]{:S(2)}) collective-permute-start(bf16[4,64,128]{2,1,0:T(8,128)(2,1)S(1)} %get-tuple-element.16), channel_id=1, source_target_pairs={{0,1},{1,0},{2,3},{3,2},{4,5},{5,4},{6,7},{7,6},{8,9},{9,8},{10,11... | collective-permute-start | bytes 196616 | tf_op jit(solution)/shard_map/ppermute | solution.py:28
  32.0 0.9 %collective-permute-done.12 = bf16[4,64,128]{2,1,0:T(8,128)(2,1)S(1)} collective-permute-done((bf16[4,64,128]{2,1,0:T(8,128)(2,1)S(1)}, bf16[4,64,128]{2,1,0:T(8,128)(2,1)S(1)}, u32[]{:S(2)}, u32[]{:S(2)}) %collective-permute-start.12) | collective-permute-done | bytes 65568 | tf_op jit(solution)/shard_map/ppermute | solution.py:28
  32.9 2.5 %collective-permute-start.13 = (bf16[4,64,128]{2,1,0:T(8,128)(2,1)S(1)}, bf16[4,64,128]{2,1,0:T(8,128)(2,1)S(1)}, u32[]{:S(2)}, u32[]{:S(2)}) collective-permute-start(bf16[4,64,128]{2,1,0:T(8,128)(2,1)S(1)} %add_convert_fusion), channel_id=1, source_target_pairs={{0,6},{2,4},{4,2},{6,0},{1,7},{3,5},{5,3},{7,1},{8,14},{10,12},{12... | collective-permute-start | bytes 196616 | tf_op jit(solution)/shard_map/ppermute | solution.py:28
  35.4 0.5 %collective-permute-start.15 = (bf16[4,64,128]{2,1,0:T(8,128)(2,1)S(1)}, bf16[4,64,128]{2,1,0:T(8,128)(2,1)S(1)}, u32[]{:S(2)}, u32[]{:S(2)}) collective-permute-start(bf16[4,64,128]{2,1,0:T(8,128)(2,1)S(1)} %add_convert_fusion), channel_id=1, source_target_pairs={{0,2},{2,0},{4,6},{6,4},{1,3},{3,1},{5,7},{7,5},{8,10},{10,8},{12,... | collective-permute-start | bytes 196616 | tf_op jit(solution)/shard_map/ppermute | solution.py:28
  36.0 0.5 %collective-permute-start.14 = (bf16[4,64,128]{2,1,0:T(8,128)(2,1)S(1)}, bf16[4,64,128]{2,1,0:T(8,128)(2,1)S(1)}, u32[]{:S(2)}, u32[]{:S(2)}) collective-permute-start(bf16[4,64,128]{2,1,0:T(8,128)(2,1)S(1)} %add_convert_fusion), channel_id=1, source_target_pairs={{0,4},{2,6},{4,0},{6,2},{1,5},{3,7},{5,1},{7,3},{8,12},{10,14},{12... | collective-permute-start | bytes 196616 | tf_op jit(solution)/shard_map/ppermute | solution.py:28
  36.5 2.0 %collective-permute-done.13.refs_0_ = bf16[4,64,128]{2,1,0:T(8,128)(2,1)S(1)} collective-permute-done((bf16[4,64,128]{2,1,0:T(8,128)(2,1)S(1)}, bf16[4,64,128]{2,1,0:T(8,128)(2,1)S(1)}, u32[]{:S(2)}, u32[]{:S(2)}) %collective-permute-start.13) | collective-permute-done | bytes 65568 | tf_op jit(solution)/shard_map/ppermute | solution.py:28
  38.5 1.2 %collective-permute-done.15 = bf16[4,64,128]{2,1,0:T(8,128)(2,1)S(1)} collective-permute-done((bf16[4,64,128]{2,1,0:T(8,128)(2,1)S(1)}, bf16[4,64,128]{2,1,0:T(8,128)(2,1)S(1)}, u32[]{:S(2)}, u32[]{:S(2)}) %collective-permute-start.15) | collective-permute-done | bytes 65568 | tf_op jit(solution)/shard_map/ppermute | solution.py:28
  39.7 0.5 %collective-permute-done.14 = bf16[4,64,128]{2,1,0:T(8,128)(2,1)S(1)} collective-permute-done((bf16[4,64,128]{2,1,0:T(8,128)(2,1)S(1)}, bf16[4,64,128]{2,1,0:T(8,128)(2,1)S(1)}, u32[]{:S(2)}, u32[]{:S(2)}) %collective-permute-start.14) | collective-permute-done | bytes 65568 | tf_op jit(solution)/shard_map/ppermute | solution.py:28
  40.2 0.7 %add_bitcast_fusion = f32[1,4,64,128]{3,2,1,0:T(8,128)} fusion(bf16[4,64,128]{2,1,0:T(8,128)(2,1)S(1)} %add_convert_fusion, bf16[4,64,128]{2,1,0:T(8,128)(2,1)S(1)} %collective-permute-done.15, bf16[4,64,128]{2,1,0:T(8,128)(2,1)S(1)} %collective-permute-done.14, bf16[4,64,128]{2,1,0:T(8,128)(2,1)S(1)} %after.5), kind=kLoop, calls=%fused_computation | loop fusion | flops 229376 | bytes 393216 | tf_op jit(solution)/shard_map/broadcast_in_dim | solution.py:375
  (5 shorter events, 0.1 us)
Async XLA Ops:
  0.8 5.6 %collective-permute-start = (bf16[32,1024]{1,0:T(8,128)(2,1)S(1)}, bf16[32,1024]{1,0:T(8,128)(2,1)S(1)}, u32[]{:S(2)}, u32[]{:S(2)}) collective-permute-start(bf16[32,1024]{1,0:T(8,128)(2,1)S(1)} %dynamic-slice_bitcast_fusion), channel_id=1, source_target_pairs={{0,8},{8,0},{16,24},{24,16},{1,9},{9,1},{17,25},{25,17},{2,10},{10... | collective-permute-start | bytes 196616 | tf_op jit(solution)/shard_map/ppermute | solution.py:28
  3.9 7.3 %collective-permute-start.1 = (bf16[32,1024]{1,0:T(8,128)(2,1)S(1)}, bf16[32,1024]{1,0:T(8,128)(2,1)S(1)}, u32[]{:S(2)}, u32[]{:S(2)}) collective-permute-start(bf16[32,1024]{1,0:T(8,128)(2,1)S(1)} %dynamic-slice_bitcast_fusion), channel_id=1, source_target_pairs={{0,16},{8,24},{16,0},{24,8},{1,17},{9,25},{17,1},{25,9},{2,18},{10... | collective-permute-start | bytes 196616 | tf_op jit(solution)/shard_map/ppermute | solution.py:28
  6.5 6.8 %collective-permute-start.3 = (bf16[32,1024]{1,0:T(8,128)(2,1)S(1)}, bf16[32,1024]{1,0:T(8,128)(2,1)S(1)}, u32[]{:S(2)}, u32[]{:S(2)}) collective-permute-start(bf16[32,1024]{1,0:T(8,128)(2,1)S(1)} %dynamic-slice_bitcast_fusion), channel_id=1, source_target_pairs={{0,24},{8,16},{16,8},{24,0},{1,25},{9,17},{17,9},{25,1},{2,26},{10... | collective-permute-start | bytes 196616 | tf_op jit(solution)/shard_map/ppermute | solution.py:28
  7.4 11.3 %collective-permute-start.4 = (bf16[512,128]{1,0:T(8,128)(2,1)S(1)}, bf16[512,128]{1,0:T(8,128)(2,1)S(1)}, u32[]{:S(2)}, u32[]{:S(2)}) collective-permute-start(bf16[512,128]{1,0:T(8,128)(2,1)S(1)} %pack.1.refs_0_), channel_id=1, source_target_pairs={{0,8},{8,0},{16,24},{24,16},{1,9},{9,1},{17,25},{25,17},{2,10},{10... | collective-permute-start | bytes 393224 | tf_op jit(solution)/shard_map/ppermute | solution.py:28
  11.2 7.5 %collective-permute-start.2 = (bf16[512,128]{1,0:T(8,128)(2,1)S(1)}, bf16[512,128]{1,0:T(8,128)(2,1)S(1)}, u32[]{:S(2)}, u32[]{:S(2)}) collective-permute-start(bf16[512,128]{1,0:T(8,128)(2,1)S(1)} %after.3), channel_id=1, source_target_pairs={{0,16},{8,24},{16,0},{24,8},{1,17},{9,25},{17,1},{25,9},{2,18},{10... | collective-permute-start | bytes 393224 | tf_op jit(solution)/shard_map/ppermute | solution.py:28
  13.2 10.2 %collective-permute-start.11 = (bf16[96,1024]{1,0:T(8,128)(2,1)S(1)}, bf16[96,1024]{1,0:T(8,128)(2,1)S(1)}, u32[]{:S(2)}, u32[]{:S(2)}) collective-permute-start(bf16[96,1024]{1,0:T(8,128)(2,1)S(1)} %join.1.refs_1_.refs_0_), channel_id=1, source_target_pairs={{0,6},{2,4},{4,2},{6,0},{1,7},{3,5},{5,3},{7,1},{8,14},{10,12},{12... | collective-permute-start | bytes 589832 | tf_op jit(solution)/shard_map/ppermute | solution.py:28
  15.8 8.4 %collective-permute-start.10 = (bf16[96,1024]{1,0:T(8,128)(2,1)S(1)}, bf16[96,1024]{1,0:T(8,128)(2,1)S(1)}, u32[]{:S(2)}, u32[]{:S(2)}) collective-permute-start(bf16[96,1024]{1,0:T(8,128)(2,1)S(1)} %join.1.refs_1_.refs_0_), channel_id=1, source_target_pairs={{0,4},{2,6},{4,0},{6,2},{1,5},{3,7},{5,1},{7,3},{8,12},{10,14},{12... | collective-permute-start | bytes 589832 | tf_op jit(solution)/shard_map/ppermute | solution.py:28
  16.3 7.9 %collective-permute-start.9 = (bf16[96,1024]{1,0:T(8,128)(2,1)S(1)}, bf16[96,1024]{1,0:T(8,128)(2,1)S(1)}, u32[]{:S(2)}, u32[]{:S(2)}) collective-permute-start(bf16[96,1024]{1,0:T(8,128)(2,1)S(1)} %join.1.refs_1_.refs_0_), channel_id=1, source_target_pairs={{0,2},{2,0},{4,6},{6,4},{1,3},{3,1},{5,7},{7,5},{8,10},{10,8},{12,... | collective-permute-start | bytes 589832 | tf_op jit(solution)/shard_map/ppermute | solution.py:28
  18.7 5.3 %collective-permute-start.7 = (bf16[512,128]{1,0:T(8,128)(2,1)S(1)}, bf16[512,128]{1,0:T(8,128)(2,1)S(1)}, u32[]{:S(2)}, u32[]{:S(2)}) collective-permute-start(bf16[512,128]{1,0:T(8,128)(2,1)S(1)} %after.4.after_ref.refs_2_), channel_id=1, source_target_pairs={{0,8},{8,0},{16,24},{24,16},{1,9},{9,1},{17,25},{25,17},{2,10},{10... | collective-permute-start | bytes 393224 | tf_op jit(solution)/shard_map/ppermute | solution.py:28
  18.8 5.4 %collective-permute-start.6 = (bf16[512,128]{1,0:T(8,128)(2,1)S(1)}, bf16[512,128]{1,0:T(8,128)(2,1)S(1)}, u32[]{:S(2)}, u32[]{:S(2)}) collective-permute-start(bf16[512,128]{1,0:T(8,128)(2,1)S(1)} %after.4.after_ref.refs_2_), channel_id=1, source_target_pairs={{0,1},{1,0},{2,3},{3,2},{4,5},{5,4},{6,7},{7,6},{8,9},{9,8},{10,11... | collective-permute-start | bytes 393224 | tf_op jit(solution)/shard_map/ppermute | solution.py:28
  23.5 1.5 %collective-permute-start.5 = (bf16[512,128]{1,0:T(8,128)(2,1)S(1)}, bf16[512,128]{1,0:T(8,128)(2,1)S(1)}, u32[]{:S(2)}, u32[]{:S(2)}) collective-permute-start(bf16[512,128]{1,0:T(8,128)(2,1)S(1)} %collective-permute-done.4.refs_2_.refs_0_), channel_id=1, source_target_pairs={{0,1},{1,0},{2,3},{3,2},{4,5},{5,4},{6,7},{7,6},{8,9},{9,8},{10,11... | collective-permute-start | bytes 393224 | tf_op jit(solution)/shard_map/ppermute | solution.py:28
  24.0 2.0 %collective-permute-start.8 = (bf16[512,128]{1,0:T(8,128)(2,1)S(1)}, bf16[512,128]{1,0:T(8,128)(2,1)S(1)}, u32[]{:S(2)}, u32[]{:S(2)}) collective-permute-start(bf16[512,128]{1,0:T(8,128)(2,1)S(1)} %collective-permute-done.7.refs_5_), channel_id=1, source_target_pairs={{0,1},{1,0},{2,3},{3,2},{4,5},{5,4},{6,7},{7,6},{8,9},{9,8},{10,11... | collective-permute-start | bytes 393224 | tf_op jit(solution)/shard_map/ppermute | solution.py:28
  31.6 1.3 %collective-permute-start.12 = (bf16[4,64,128]{2,1,0:T(8,128)(2,1)S(1)}, bf16[4,64,128]{2,1,0:T(8,128)(2,1)S(1)}, u32[]{:S(2)}, u32[]{:S(2)}) collective-permute-start(bf16[4,64,128]{2,1,0:T(8,128)(2,1)S(1)} %get-tuple-element.16), channel_id=1, source_target_pairs={{0,1},{1,0},{2,3},{3,2},{4,5},{5,4},{6,7},{7,6},{8,9},{9,8},{10,11... | collective-permute-start | bytes 196616 | tf_op jit(solution)/shard_map/ppermute | solution.py:28
  32.9 5.6 %collective-permute-start.13 = (bf16[4,64,128]{2,1,0:T(8,128)(2,1)S(1)}, bf16[4,64,128]{2,1,0:T(8,128)(2,1)S(1)}, u32[]{:S(2)}, u32[]{:S(2)}) collective-permute-start(bf16[4,64,128]{2,1,0:T(8,128)(2,1)S(1)} %add_convert_fusion), channel_id=1, source_target_pairs={{0,6},{2,4},{4,2},{6,0},{1,7},{3,5},{5,3},{7,1},{8,14},{10,12},{12... | collective-permute-start | bytes 196616 | tf_op jit(solution)/shard_map/ppermute | solution.py:28
  35.4 4.3 %collective-permute-start.15 = (bf16[4,64,128]{2,1,0:T(8,128)(2,1)S(1)}, bf16[4,64,128]{2,1,0:T(8,128)(2,1)S(1)}, u32[]{:S(2)}, u32[]{:S(2)}) collective-permute-start(bf16[4,64,128]{2,1,0:T(8,128)(2,1)S(1)} %add_convert_fusion), channel_id=1, source_target_pairs={{0,2},{2,0},{4,6},{6,4},{1,3},{3,1},{5,7},{7,5},{8,10},{10,8},{12,... | collective-permute-start | bytes 196616 | tf_op jit(solution)/shard_map/ppermute | solution.py:28
  36.0 4.3 %collective-permute-start.14 = (bf16[4,64,128]{2,1,0:T(8,128)(2,1)S(1)}, bf16[4,64,128]{2,1,0:T(8,128)(2,1)S(1)}, u32[]{:S(2)}, u32[]{:S(2)}) collective-permute-start(bf16[4,64,128]{2,1,0:T(8,128)(2,1)S(1)} %add_convert_fusion), channel_id=1, source_target_pairs={{0,4},{2,6},{4,0},{6,2},{1,5},{3,7},{5,1},{7,3},{8,12},{10,14},{12... | collective-permute-start | bytes 196616 | tf_op jit(solution)/shard_map/ppermute | solution.py:28

commit v4 on v0

--- a/solution.py
+++ b/solution.py
@@ -104,7 +104,7 @@
     ]
     for copy in copies:
         copy.start()
-    for copy in copies[:4]:
+    for copy in copies[:3]:
         copy.wait()
     n_v, n_nu = val.shape
     n_b = exciton.shape[0] // n_v
@@ -113,6 +113,8 @@
         for j in range(n_nu // CHUNK):
             at = slice(j * CHUNK, (j + 1) * CHUNK)
             product = jnp.dot(panels[t % 2], val[:, at], preferred_element_type=F32)
+            if t == 0 and j == 0:
+                copies[3].wait()
             weights = w_own[t * TILE:(t + 1) * TILE, at].astype(F32)
             for b in range(n_b):
                 rows = slice(b * TILE, (b + 1) * TILE)
@@ -213,16 +215,21 @@
                     value += products[number % 2, i, rows, :].astype(F32) * weights[i]
                 direct[t % 2, rows, at] = value.astype(BF16)
 
+    per_tile = n_nu // CHUNK
+    span = 2 if per_tile % 2 == 0 else 1
+
     def reduce(number):
         t, j = steps[number]
-        at = slice(j * CHUNK, (j + 1) * CHUNK)
+        if (j + 1) % span:
+            return
+        at = slice((j + 1 - span) * CHUNK, (j + 1) * CHUNK)
         value = lax.dot_general(
             direct[t % 2, :, at], val_own[:, at], (((1,), (1,)), ((), ())),
             preferred_element_type=F32,
         )
-        if j:
+        if j + 1 > span:
             value += running[...]
-        if j + 1 < n_nu // CHUNK:
+        if j + 1 < per_tile:
             running[...] = value
             return
         value = value.astype(BF16)

time: 39.9 us -> 40.1 us (level)
  no operation moved by 1% of the time
where the time goes in v4:
time: 40.1 us; the launch traced here: 39.8 us
  starting transfers between devices  16.7 us (42%)
  Pallas kernels  10.9 us (27%)
  waiting for transfers between devices  10.6 us (26%)
  local copies, waits for them, and re-layouts  0.84 us (2%)
  other arithmetic  0.71 us (2%)
    ppermute x16, starting transfers between devices, swap(): return lax.ppermute(value, axis, [(i, i ^ flip) for i in range(size)])  16.7 us
    ppermute x16, waiting for transfers between devices, swap(): return lax.ppermute(value, axis, [(i, i ^ flip) for i in range(size)])  10.6 us
    pallas_call x1, Pallas kernels, local(): pl.pallas_call(functools.partial(direct_kernel, sizes, early, factor), in...  5.39 us
    pallas_call x1, Pallas kernels, local(): pl.pallas_call(own_kernel, in_specs=[IN_SMEM] + [IN_HBM] * 4 + [pl.BlockS...  3.95 us
    pallas_call x1, Pallas kernels, local(): pl.pallas_call(functools.partial(pack_kernel, n_col), in_specs=[IN_HBM] *...  0.95 us
    dynamic_slice x1, local copies, waits for them, and re-layouts, local(): lax.dynamic_slice_in_dim(orb_val[0], lax.axis_index('row') * part, part, 0)  0.84 us
  transfers between devices with their start and end apart: 16, of which 10 were waited for; matrix products, arithmetic and copies ran while one was open for 0% of the time, Pallas kernels for 14%

profile of v4, /device:TPU:0, one launch (start us, length us, event | category | flops | bytes accessed | tf_op | source)
XLA Modules:
  0.0 39.8 jit_solution(2659367608783226499)
XLA Ops:
  0.0 0.8 %dynamic-slice_bitcast_fusion = bf16[32,1024]{1,0:T(8,128)(2,1)S(1)} fusion(bf16[1,128,1024]{2,1,0:T(8,128)(2,1)} %param.7, s32[]{:T(128)S(6)} %select_n.3), kind=kLoop, calls=%fused_computation.2 | loop fusion | bytes 131076 | tf_op jit(solution)/shard_map/dynamic_slice | solution.py:277
  0.8 3.0 %collective-permute-start = (bf16[32,1024]{1,0:T(8,128)(2,1)S(1)}, bf16[32,1024]{1,0:T(8,128)(2,1)S(1)}, u32[]{:S(2)}, u32[]{:S(2)}) collective-permute-start(bf16[32,1024]{1,0:T(8,128)(2,1)S(1)} %dynamic-slice_bitcast_fusion), channel_id=1, source_target_pairs={{0,8},{8,0},{16,24},{24,16},{1,9},{9,1},{17,25},{25,17},{2,10},{10... | collective-permute-start | bytes 196616 | tf_op jit(solution)/shard_map/ppermute | solution.py:28
  3.9 2.6 %collective-permute-start.1 = (bf16[32,1024]{1,0:T(8,128)(2,1)S(1)}, bf16[32,1024]{1,0:T(8,128)(2,1)S(1)}, u32[]{:S(2)}, u32[]{:S(2)}) collective-permute-start(bf16[32,1024]{1,0:T(8,128)(2,1)S(1)} %dynamic-slice_bitcast_fusion), channel_id=1, source_target_pairs={{0,16},{8,24},{16,0},{24,8},{1,17},{9,25},{17,1},{25,9},{2,18},{10... | collective-permute-start | bytes 196616 | tf_op jit(solution)/shard_map/ppermute | solution.py:28
  6.5 0.0 collective-permute-start.3
  6.5 0.0 collective-permute-done.after_ref.refs_0_
  6.5 1.0 %pack.1.refs_0_ = bf16[512,128]{1,0:T(8,128)(2,1)S(1)} custom-call(bf16[512,128]{1,0:T(8,128)(2,1)} %bitcast.7, bf16[128,512]{1,0:T(8,128)(2,1)} %bitcast.9, bf16[32,1024]{1,0:T(8,128)(2,1)S(1)} %collective-permute-done.after_ref.refs_0_), custom_call_target="tpu_custom_call" | custom-call | tf_op jit(solution)/shard_map/pack/pallas_call | solution.py:279
  7.4 1.7 %collective-permute-start.4 = (bf16[512,128]{1,0:T(8,128)(2,1)S(1)}, bf16[512,128]{1,0:T(8,128)(2,1)S(1)}, u32[]{:S(2)}, u32[]{:S(2)}) collective-permute-start(bf16[512,128]{1,0:T(8,128)(2,1)S(1)} %pack.1.refs_0_), channel_id=1, source_target_pairs={{0,8},{8,0},{16,24},{24,16},{1,9},{9,1},{17,25},{25,17},{2,10},{10... | collective-permute-start | bytes 393224 | tf_op jit(solution)/shard_map/ppermute | solution.py:28
  9.2 2.0 %collective-permute-done.1.refs_1_ = bf16[32,1024]{1,0:T(8,128)(2,1)S(1)} collective-permute-done((bf16[32,1024]{1,0:T(8,128)(2,1)S(1)}, bf16[32,1024]{1,0:T(8,128)(2,1)S(1)}, u32[]{:S(2)}, u32[]{:S(2)}) %collective-permute-start.1) | collective-permute-done | bytes 65568 | tf_op jit(solution)/shard_map/ppermute | solution.py:28
  11.2 1.3 %collective-permute-start.2 = (bf16[512,128]{1,0:T(8,128)(2,1)S(1)}, bf16[512,128]{1,0:T(8,128)(2,1)S(1)}, u32[]{:S(2)}, u32[]{:S(2)}) collective-permute-start(bf16[512,128]{1,0:T(8,128)(2,1)S(1)} %after.3), channel_id=1, source_target_pairs={{0,16},{8,24},{16,0},{24,8},{1,17},{9,25},{17,1},{25,9},{2,18},{10... | collective-permute-start | bytes 393224 | tf_op jit(solution)/shard_map/ppermute | solution.py:28
  12.5 0.8 %collective-permute-done.3.refs_2_ = bf16[32,1024]{1,0:T(8,128)(2,1)S(1)} collective-permute-done((bf16[32,1024]{1,0:T(8,128)(2,1)S(1)}, bf16[32,1024]{1,0:T(8,128)(2,1)S(1)}, u32[]{:S(2)}, u32[]{:S(2)}) %collective-permute-start.3) | collective-permute-done | bytes 65568 | tf_op jit(solution)/shard_map/ppermute | solution.py:28
  13.2 2.5 %collective-permute-start.11 = (bf16[96,1024]{1,0:T(8,128)(2,1)S(1)}, bf16[96,1024]{1,0:T(8,128)(2,1)S(1)}, u32[]{:S(2)}, u32[]{:S(2)}) collective-permute-start(bf16[96,1024]{1,0:T(8,128)(2,1)S(1)} %join.1.refs_1_.refs_0_), channel_id=1, source_target_pairs={{0,6},{2,4},{4,2},{6,0},{1,7},{3,5},{5,3},{7,1},{8,14},{10,12},{12... | collective-permute-start | bytes 589832 | tf_op jit(solution)/shard_map/ppermute | solution.py:28
  15.8 0.5 %collective-permute-start.10 = (bf16[96,1024]{1,0:T(8,128)(2,1)S(1)}, bf16[96,1024]{1,0:T(8,128)(2,1)S(1)}, u32[]{:S(2)}, u32[]{:S(2)}) collective-permute-start(bf16[96,1024]{1,0:T(8,128)(2,1)S(1)} %join.1.refs_1_.refs_0_), channel_id=1, source_target_pairs={{0,4},{2,6},{4,0},{6,2},{1,5},{3,7},{5,1},{7,3},{8,12},{10,14},{12... | collective-permute-start | bytes 589832 | tf_op jit(solution)/shard_map/ppermute | solution.py:28
  16.3 0.5 %collective-permute-start.9 = (bf16[96,1024]{1,0:T(8,128)(2,1)S(1)}, bf16[96,1024]{1,0:T(8,128)(2,1)S(1)}, u32[]{:S(2)}, u32[]{:S(2)}) collective-permute-start(bf16[96,1024]{1,0:T(8,128)(2,1)S(1)} %join.1.refs_1_.refs_0_), channel_id=1, source_target_pairs={{0,2},{2,0},{4,6},{6,4},{1,3},{3,1},{5,7},{7,5},{8,10},{10,8},{12,... | collective-permute-start | bytes 589832 | tf_op jit(solution)/shard_map/ppermute | solution.py:28
  16.8 1.9 %collective-permute-done.2.refs_0_ = bf16[512,128]{1,0:T(8,128)(2,1)S(1)} collective-permute-done((bf16[512,128]{1,0:T(8,128)(2,1)S(1)}, bf16[512,128]{1,0:T(8,128)(2,1)S(1)}, u32[]{:S(2)}, u32[]{:S(2)}) %collective-permute-start.2) | collective-permute-done | bytes 131104 | tf_op jit(solution)/shard_map/ppermute | solution.py:28
  18.7 0.0 collective-permute-done.4.refs_2_.refs_0_
  18.7 0.1 collective-permute-start.7
  18.8 0.1 collective-permute-start.6
  18.9 3.9 %own_term.1 = (f32[4,512,1024]{2,1,0:T(8,128)S(1)}, bf16[3,512,1024]{2,1,0:T(8,128)(2,1)S(1)}, bf16[128,512]{1,0:T(8,128)(2,1)S(1)}, bf16[128,1024]{1,0:T(8,128)(2,1)S(1)}) custom-call(s32[4,4]{1,0:T(4,128)} %q_ref.1, bf16[4,512,1024]{2,1,0:T(8,128)(2,1)} %w_ref.1, bf16[512,128]{1,0:T(8,128)(2,1)} %bitcast.8, bf16[128,512]{1,0:T(8,128)(2,1)} %bitcast.10, ...), custom_call_target="tpu_custom_call" | custom-call | bytes 8388608 | tf_op jit(solution)/shard_map/own_term/pallas_call | solution.py:299
  22.8 0.0 collective-permute-done.11.refs_3_
  22.8 0.5 %collective-permute-start.5 = (bf16[512,128]{1,0:T(8,128)(2,1)S(1)}, bf16[512,128]{1,0:T(8,128)(2,1)S(1)}, u32[]{:S(2)}, u32[]{:S(2)}) collective-permute-start(bf16[512,128]{1,0:T(8,128)(2,1)S(1)} %collective-permute-done.4.refs_2_.refs_0_), channel_id=1, source_target_pairs={{0,1},{1,0},{2,3},{3,2},{4,5},{5,4},{6,7},{7,6},{8,9},{9,8},{10,11... | collective-permute-start | bytes 393224 | tf_op jit(solution)/shard_map/ppermute | solution.py:28
  23.4 0.4 collective-permute-done.7.refs_5_
  23.7 0.0 collective-permute-start.8
  23.7 0.0 collective-permute-done.10.refs_2_
  23.7 0.0 collective-permute-done.9.refs_1_
  23.7 0.1 spread.1.refs_7_
  23.8 0.0 collective-permute-done.6.refs_3_
  23.8 0.5 %collective-permute-done.5.refs_1_ = bf16[512,128]{1,0:T(8,128)(2,1)S(1)} collective-permute-done((bf16[512,128]{1,0:T(8,128)(2,1)S(1)}, bf16[512,128]{1,0:T(8,128)(2,1)S(1)}, u32[]{:S(2)}, u32[]{:S(2)}) %collective-permute-start.5) | collective-permute-done | bytes 131104 | tf_op jit(solution)/shard_map/ppermute | solution.py:28
  24.4 0.5 %panels.1.refs_4_ = bf16[2,4,512,128]{3,2,1,0:T(8,128)(2,1)S(1)} custom-call(bf16[512,128]{1,0:T(8,128)(2,1)S(1)} %collective-permute-done.4.refs_2_.refs_0_, bf16[512,128]{1,0:T(8,128)(2,1)S(1)} %collective-permute-done.5.refs_1_, bf16[512,128]{1,0:T(8,128)(2,1)S(1)} %after.4.after_ref.refs_2_, bf16[512,128]{1,0:T(8,128)(2,1)S(1)} %collective-permute-done.6.refs_3_), custom_call_target="tpu_custom_call" | custom-call | flops 1000000000 | tf_op jit(solution)/shard_map/panels/pallas_call | solution.py:326
  24.9 0.2 collective-permute-done.8.refs_6_
  25.1 5.4 %direct_term.1 = (f32[4,64,128]{2,1,0:T(8,128)S(1)}, bf16[4,64,128]{2,1,0:T(8,128)(2,1)S(1)}) custom-call(f32[4,512,1024]{2,1,0:T(8,128)S(1)} %get-tuple-element.11.refs_0_, bf16[3,512,1024]{2,1,0:T(8,128)(2,1)S(1)} %get-tuple-element.12.refs_1_, bf16[128,512]{1,0:T(8,128)(2,1)S(1)} %get-tuple-element.13.refs_2_, ...), custom_call_target="tpu_custom_call" | custom-call | tf_op jit(solution)/shard_map/direct_term/pallas_call | solution.py:354
  30.5 0.2 collective-permute-start.12
  30.7 1.1 %collective-permute-done.12 = bf16[4,64,128]{2,1,0:T(8,128)(2,1)S(1)} collective-permute-done((bf16[4,64,128]{2,1,0:T(8,128)(2,1)S(1)}, bf16[4,64,128]{2,1,0:T(8,128)(2,1)S(1)}, u32[]{:S(2)}, u32[]{:S(2)}) %collective-permute-start.12) | collective-permute-done | bytes 65568 | tf_op jit(solution)/shard_map/ppermute | solution.py:28
  31.8 2.5 %collective-permute-start.13 = (bf16[4,64,128]{2,1,0:T(8,128)(2,1)S(1)}, bf16[4,64,128]{2,1,0:T(8,128)(2,1)S(1)}, u32[]{:S(2)}, u32[]{:S(2)}) collective-permute-start(bf16[4,64,128]{2,1,0:T(8,128)(2,1)S(1)} %add_convert_fusion), channel_id=1, source_target_pairs={{0,6},{2,4},{4,2},{6,0},{1,7},{3,5},{5,3},{7,1},{8,14},{10,12},{12... | collective-permute-start | bytes 196616 | tf_op jit(solution)/shard_map/ppermute | solution.py:28
  34.3 0.5 %collective-permute-start.15 = (bf16[4,64,128]{2,1,0:T(8,128)(2,1)S(1)}, bf16[4,64,128]{2,1,0:T(8,128)(2,1)S(1)}, u32[]{:S(2)}, u32[]{:S(2)}) collective-permute-start(bf16[4,64,128]{2,1,0:T(8,128)(2,1)S(1)} %add_convert_fusion), channel_id=1, source_target_pairs={{0,2},{2,0},{4,6},{6,4},{1,3},{3,1},{5,7},{7,5},{8,10},{10,8},{12,... | collective-permute-start | bytes 196616 | tf_op jit(solution)/shard_map/ppermute | solution.py:28
  34.9 0.5 %collective-permute-start.14 = (bf16[4,64,128]{2,1,0:T(8,128)(2,1)S(1)}, bf16[4,64,128]{2,1,0:T(8,128)(2,1)S(1)}, u32[]{:S(2)}, u32[]{:S(2)}) collective-permute-start(bf16[4,64,128]{2,1,0:T(8,128)(2,1)S(1)} %add_convert_fusion), channel_id=1, source_target_pairs={{0,4},{2,6},{4,0},{6,2},{1,5},{3,7},{5,1},{7,3},{8,12},{10,14},{12... | collective-permute-start | bytes 196616 | tf_op jit(solution)/shard_map/ppermute | solution.py:28
  35.4 2.0 %collective-permute-done.13.refs_0_ = bf16[4,64,128]{2,1,0:T(8,128)(2,1)S(1)} collective-permute-done((bf16[4,64,128]{2,1,0:T(8,128)(2,1)S(1)}, bf16[4,64,128]{2,1,0:T(8,128)(2,1)S(1)}, u32[]{:S(2)}, u32[]{:S(2)}) %collective-permute-start.13) | collective-permute-done | bytes 65568 | tf_op jit(solution)/shard_map/ppermute | solution.py:28
  37.4 1.2 %collective-permute-done.15 = bf16[4,64,128]{2,1,0:T(8,128)(2,1)S(1)} collective-permute-done((bf16[4,64,128]{2,1,0:T(8,128)(2,1)S(1)}, bf16[4,64,128]{2,1,0:T(8,128)(2,1)S(1)}, u32[]{:S(2)}, u32[]{:S(2)}) %collective-permute-start.15) | collective-permute-done | bytes 65568 | tf_op jit(solution)/shard_map/ppermute | solution.py:28
  38.6 0.5 %collective-permute-done.14 = bf16[4,64,128]{2,1,0:T(8,128)(2,1)S(1)} collective-permute-done((bf16[4,64,128]{2,1,0:T(8,128)(2,1)S(1)}, bf16[4,64,128]{2,1,0:T(8,128)(2,1)S(1)}, u32[]{:S(2)}, u32[]{:S(2)}) %collective-permute-start.14) | collective-permute-done | bytes 65568 | tf_op jit(solution)/shard_map/ppermute | solution.py:28
  39.1 0.7 %add_bitcast_fusion = f32[1,4,64,128]{3,2,1,0:T(8,128)} fusion(bf16[4,64,128]{2,1,0:T(8,128)(2,1)S(1)} %add_convert_fusion, bf16[4,64,128]{2,1,0:T(8,128)(2,1)S(1)} %collective-permute-done.15, bf16[4,64,128]{2,1,0:T(8,128)(2,1)S(1)} %collective-permute-done.14, bf16[4,64,128]{2,1,0:T(8,128)(2,1)S(1)} %after.5), kind=kLoop, calls=%fused_computation | loop fusion | flops 229376 | bytes 393216 | tf_op jit(solution)/shard_map/broadcast_in_dim | solution.py:382
  (5 shorter events, 0.1 us)
Async XLA Ops:
  0.8 5.6 %collective-permute-start = (bf16[32,1024]{1,0:T(8,128)(2,1)S(1)}, bf16[32,1024]{1,0:T(8,128)(2,1)S(1)}, u32[]{:S(2)}, u32[]{:S(2)}) collective-permute-start(bf16[32,1024]{1,0:T(8,128)(2,1)S(1)} %dynamic-slice_bitcast_fusion), channel_id=1, source_target_pairs={{0,8},{8,0},{16,24},{24,16},{1,9},{9,1},{17,25},{25,17},{2,10},{10... | collective-permute-start | bytes 196616 | tf_op jit(solution)/shard_map/ppermute | solution.py:28
  3.9 7.3 %collective-permute-start.1 = (bf16[32,1024]{1,0:T(8,128)(2,1)S(1)}, bf16[32,1024]{1,0:T(8,128)(2,1)S(1)}, u32[]{:S(2)}, u32[]{:S(2)}) collective-permute-start(bf16[32,1024]{1,0:T(8,128)(2,1)S(1)} %dynamic-slice_bitcast_fusion), channel_id=1, source_target_pairs={{0,16},{8,24},{16,0},{24,8},{1,17},{9,25},{17,1},{25,9},{2,18},{10... | collective-permute-start | bytes 196616 | tf_op jit(solution)/shard_map/ppermute | solution.py:28
  6.5 6.8 %collective-permute-start.3 = (bf16[32,1024]{1,0:T(8,128)(2,1)S(1)}, bf16[32,1024]{1,0:T(8,128)(2,1)S(1)}, u32[]{:S(2)}, u32[]{:S(2)}) collective-permute-start(bf16[32,1024]{1,0:T(8,128)(2,1)S(1)} %dynamic-slice_bitcast_fusion), channel_id=1, source_target_pairs={{0,24},{8,16},{16,8},{24,0},{1,25},{9,17},{17,9},{25,1},{2,26},{10... | collective-permute-start | bytes 196616 | tf_op jit(solution)/shard_map/ppermute | solution.py:28
  7.4 11.3 %collective-permute-start.4 = (bf16[512,128]{1,0:T(8,128)(2,1)S(1)}, bf16[512,128]{1,0:T(8,128)(2,1)S(1)}, u32[]{:S(2)}, u32[]{:S(2)}) collective-permute-start(bf16[512,128]{1,0:T(8,128)(2,1)S(1)} %pack.1.refs_0_), channel_id=1, source_target_pairs={{0,8},{8,0},{16,24},{24,16},{1,9},{9,1},{17,25},{25,17},{2,10},{10... | collective-permute-start | bytes 393224 | tf_op jit(solution)/shard_map/ppermute | solution.py:28
  11.2 7.5 %collective-permute-start.2 = (bf16[512,128]{1,0:T(8,128)(2,1)S(1)}, bf16[512,128]{1,0:T(8,128)(2,1)S(1)}, u32[]{:S(2)}, u32[]{:S(2)}) collective-permute-start(bf16[512,128]{1,0:T(8,128)(2,1)S(1)} %after.3), channel_id=1, source_target_pairs={{0,16},{8,24},{16,0},{24,8},{1,17},{9,25},{17,1},{25,9},{2,18},{10... | collective-permute-start | bytes 393224 | tf_op jit(solution)/shard_map/ppermute | solution.py:28
  13.2 9.6 %collective-permute-start.11 = (bf16[96,1024]{1,0:T(8,128)(2,1)S(1)}, bf16[96,1024]{1,0:T(8,128)(2,1)S(1)}, u32[]{:S(2)}, u32[]{:S(2)}) collective-permute-start(bf16[96,1024]{1,0:T(8,128)(2,1)S(1)} %join.1.refs_1_.refs_0_), channel_id=1, source_target_pairs={{0,6},{2,4},{4,2},{6,0},{1,7},{3,5},{5,3},{7,1},{8,14},{10,12},{12... | collective-permute-start | bytes 589832 | tf_op jit(solution)/shard_map/ppermute | solution.py:28
  15.8 8.0 %collective-permute-start.10 = (bf16[96,1024]{1,0:T(8,128)(2,1)S(1)}, bf16[96,1024]{1,0:T(8,128)(2,1)S(1)}, u32[]{:S(2)}, u32[]{:S(2)}) collective-permute-start(bf16[96,1024]{1,0:T(8,128)(2,1)S(1)} %join.1.refs_1_.refs_0_), channel_id=1, source_target_pairs={{0,4},{2,6},{4,0},{6,2},{1,5},{3,7},{5,1},{7,3},{8,12},{10,14},{12... | collective-permute-start | bytes 589832 | tf_op jit(solution)/shard_map/ppermute | solution.py:28
  16.3 7.5 %collective-permute-start.9 = (bf16[96,1024]{1,0:T(8,128)(2,1)S(1)}, bf16[96,1024]{1,0:T(8,128)(2,1)S(1)}, u32[]{:S(2)}, u32[]{:S(2)}) collective-permute-start(bf16[96,1024]{1,0:T(8,128)(2,1)S(1)} %join.1.refs_1_.refs_0_), channel_id=1, source_target_pairs={{0,2},{2,0},{4,6},{6,4},{1,3},{3,1},{5,7},{7,5},{8,10},{10,8},{12,... | collective-permute-start | bytes 589832 | tf_op jit(solution)/shard_map/ppermute | solution.py:28
  18.7 5.0 %collective-permute-start.7 = (bf16[512,128]{1,0:T(8,128)(2,1)S(1)}, bf16[512,128]{1,0:T(8,128)(2,1)S(1)}, u32[]{:S(2)}, u32[]{:S(2)}) collective-permute-start(bf16[512,128]{1,0:T(8,128)(2,1)S(1)} %after.4.after_ref.refs_2_), channel_id=1, source_target_pairs={{0,8},{8,0},{16,24},{24,16},{1,9},{9,1},{17,25},{25,17},{2,10},{10... | collective-permute-start | bytes 393224 | tf_op jit(solution)/shard_map/ppermute | solution.py:28
  18.8 5.0 %collective-permute-start.6 = (bf16[512,128]{1,0:T(8,128)(2,1)S(1)}, bf16[512,128]{1,0:T(8,128)(2,1)S(1)}, u32[]{:S(2)}, u32[]{:S(2)}) collective-permute-start(bf16[512,128]{1,0:T(8,128)(2,1)S(1)} %after.4.after_ref.refs_2_), channel_id=1, source_target_pairs={{0,1},{1,0},{2,3},{3,2},{4,5},{5,4},{6,7},{7,6},{8,9},{9,8},{10,11... | collective-permute-start | bytes 393224 | tf_op jit(solution)/shard_map/ppermute | solution.py:28
  22.8 1.5 %collective-permute-start.5 = (bf16[512,128]{1,0:T(8,128)(2,1)S(1)}, bf16[512,128]{1,0:T(8,128)(2,1)S(1)}, u32[]{:S(2)}, u32[]{:S(2)}) collective-permute-start(bf16[512,128]{1,0:T(8,128)(2,1)S(1)} %collective-permute-done.4.refs_2_.refs_0_), channel_id=1, source_target_pairs={{0,1},{1,0},{2,3},{3,2},{4,5},{5,4},{6,7},{7,6},{8,9},{9,8},{10,11... | collective-permute-start | bytes 393224 | tf_op jit(solution)/shard_map/ppermute | solution.py:28
  23.7 1.3 %collective-permute-start.8 = (bf16[512,128]{1,0:T(8,128)(2,1)S(1)}, bf16[512,128]{1,0:T(8,128)(2,1)S(1)}, u32[]{:S(2)}, u32[]{:S(2)}) collective-permute-start(bf16[512,128]{1,0:T(8,128)(2,1)S(1)} %collective-permute-done.7.refs_5_), channel_id=1, source_target_pairs={{0,1},{1,0},{2,3},{3,2},{4,5},{5,4},{6,7},{7,6},{8,9},{9,8},{10,11... | collective-permute-start | bytes 393224 | tf_op jit(solution)/shard_map/ppermute | solution.py:28
  30.5 1.3 %collective-permute-start.12 = (bf16[4,64,128]{2,1,0:T(8,128)(2,1)S(1)}, bf16[4,64,128]{2,1,0:T(8,128)(2,1)S(1)}, u32[]{:S(2)}, u32[]{:S(2)}) collective-permute-start(bf16[4,64,128]{2,1,0:T(8,128)(2,1)S(1)} %get-tuple-element.16), channel_id=1, source_target_pairs={{0,1},{1,0},{2,3},{3,2},{4,5},{5,4},{6,7},{7,6},{8,9},{9,8},{10,11... | collective-permute-start | bytes 196616 | tf_op jit(solution)/shard_map/ppermute | solution.py:28
  31.8 5.6 %collective-permute-start.13 = (bf16[4,64,128]{2,1,0:T(8,128)(2,1)S(1)}, bf16[4,64,128]{2,1,0:T(8,128)(2,1)S(1)}, u32[]{:S(2)}, u32[]{:S(2)}) collective-permute-start(bf16[4,64,128]{2,1,0:T(8,128)(2,1)S(1)} %add_convert_fusion), channel_id=1, source_target_pairs={{0,6},{2,4},{4,2},{6,0},{1,7},{3,5},{5,3},{7,1},{8,14},{10,12},{12... | collective-permute-start | bytes 196616 | tf_op jit(solution)/shard_map/ppermute | solution.py:28
  34.3 4.3 %collective-permute-start.15 = (bf16[4,64,128]{2,1,0:T(8,128)(2,1)S(1)}, bf16[4,64,128]{2,1,0:T(8,128)(2,1)S(1)}, u32[]{:S(2)}, u32[]{:S(2)}) collective-permute-start(bf16[4,64,128]{2,1,0:T(8,128)(2,1)S(1)} %add_convert_fusion), channel_id=1, source_target_pairs={{0,2},{2,0},{4,6},{6,4},{1,3},{3,1},{5,7},{7,5},{8,10},{10,8},{12,... | collective-permute-start | bytes 196616 | tf_op jit(solution)/shard_map/ppermute | solution.py:28
  34.9 4.3 %collective-permute-start.14 = (bf16[4,64,128]{2,1,0:T(8,128)(2,1)S(1)}, bf16[4,64,128]{2,1,0:T(8,128)(2,1)S(1)}, u32[]{:S(2)}, u32[]{:S(2)}) collective-permute-start(bf16[4,64,128]{2,1,0:T(8,128)(2,1)S(1)} %add_convert_fusion), channel_id=1, source_target_pairs={{0,4},{2,6},{4,0},{6,2},{1,5},{3,7},{5,1},{7,3},{8,12},{10,14},{12... | collective-permute-start | bytes 196616 | tf_op jit(solution)/shard_map/ppermute | solution.py:28

commit v5 on v0

--- a/solution.py
+++ b/solution.py
@@ -104,7 +104,7 @@
     ]
     for copy in copies:
         copy.start()
-    for copy in copies[:4]:
+    for copy in copies[:3]:
         copy.wait()
     n_v, n_nu = val.shape
     n_b = exciton.shape[0] // n_v
@@ -113,6 +113,8 @@
         for j in range(n_nu // CHUNK):
             at = slice(j * CHUNK, (j + 1) * CHUNK)
             product = jnp.dot(panels[t % 2], val[:, at], preferred_element_type=F32)
+            if t == 0 and j == 0:
+                copies[3].wait()
             weights = w_own[t * TILE:(t + 1) * TILE, at].astype(F32)
             for b in range(n_b):
                 rows = slice(b * TILE, (b + 1) * TILE)

time: 39.9 us -> 39.9 us (level)
  no operation moved by 1% of the time
where the time goes in v5:
time: 39.9 us; the launch traced here: 39.7 us
  starting transfers between devices  16.7 us (42%)
  Pallas kernels  10.7 us (27%)
  waiting for transfers between devices  10.6 us (27%)
  local copies, waits for them, and re-layouts  0.84 us (2%)
  other arithmetic  0.71 us (2%)
    ppermute x16, starting transfers between devices, swap(): return lax.ppermute(value, axis, [(i, i ^ flip) for i in range(size)])  16.7 us
    ppermute x16, waiting for transfers between devices, swap(): return lax.ppermute(value, axis, [(i, i ^ flip) for i in range(size)])  10.6 us
    pallas_call x1, Pallas kernels, local(): pl.pallas_call(functools.partial(direct_kernel, sizes, early, factor), in...  5.24 us
    pallas_call x1, Pallas kernels, local(): pl.pallas_call(own_kernel, in_specs=[IN_SMEM] + [IN_HBM] * 4 + [pl.BlockS...  3.95 us
    pallas_call x1, Pallas kernels, local(): pl.pallas_call(functools.partial(pack_kernel, n_col), in_specs=[IN_HBM] *...  0.95 us
    dynamic_slice x1, local copies, waits for them, and re-layouts, local(): lax.dynamic_slice_in_dim(orb_val[0], lax.axis_index('row') * part, part, 0)  0.84 us
  transfers between devices with their start and end apart: 16, of which 10 were waited for; matrix products, arithmetic and copies ran while one was open for 0% of the time, Pallas kernels for 14%

profile of v5, /device:TPU:0, one launch (start us, length us, event | category | flops | bytes accessed | tf_op | source)
XLA Modules:
  0.0 39.7 jit_solution(6425046894939501250)
XLA Ops:
  0.0 0.8 %dynamic-slice_bitcast_fusion = bf16[32,1024]{1,0:T(8,128)(2,1)S(1)} fusion(bf16[1,128,1024]{2,1,0:T(8,128)(2,1)} %param.7, s32[]{:T(128)S(6)} %select_n.3), kind=kLoop, calls=%fused_computation.2 | loop fusion | bytes 131076 | tf_op jit(solution)/shard_map/dynamic_slice | solution.py:272
  0.8 3.0 %collective-permute-start = (bf16[32,1024]{1,0:T(8,128)(2,1)S(1)}, bf16[32,1024]{1,0:T(8,128)(2,1)S(1)}, u32[]{:S(2)}, u32[]{:S(2)}) collective-permute-start(bf16[32,1024]{1,0:T(8,128)(2,1)S(1)} %dynamic-slice_bitcast_fusion), channel_id=1, source_target_pairs={{0,8},{8,0},{16,24},{24,16},{1,9},{9,1},{17,25},{25,17},{2,10},{10... | collective-permute-start | bytes 196616 | tf_op jit(solution)/shard_map/ppermute | solution.py:28
  3.9 2.6 %collective-permute-start.1 = (bf16[32,1024]{1,0:T(8,128)(2,1)S(1)}, bf16[32,1024]{1,0:T(8,128)(2,1)S(1)}, u32[]{:S(2)}, u32[]{:S(2)}) collective-permute-start(bf16[32,1024]{1,0:T(8,128)(2,1)S(1)} %dynamic-slice_bitcast_fusion), channel_id=1, source_target_pairs={{0,16},{8,24},{16,0},{24,8},{1,17},{9,25},{17,1},{25,9},{2,18},{10... | collective-permute-start | bytes 196616 | tf_op jit(solution)/shard_map/ppermute | solution.py:28
  6.5 0.0 collective-permute-start.3
  6.5 0.0 collective-permute-done.after_ref.refs_0_
  6.5 1.0 %pack.1.refs_0_ = bf16[512,128]{1,0:T(8,128)(2,1)S(1)} custom-call(bf16[512,128]{1,0:T(8,128)(2,1)} %bitcast.7, bf16[128,512]{1,0:T(8,128)(2,1)} %bitcast.9, bf16[32,1024]{1,0:T(8,128)(2,1)S(1)} %collective-permute-done.after_ref.refs_0_), custom_call_target="tpu_custom_call" | custom-call | tf_op jit(solution)/shard_map/pack/pallas_call | solution.py:274
  7.4 1.7 %collective-permute-start.4 = (bf16[512,128]{1,0:T(8,128)(2,1)S(1)}, bf16[512,128]{1,0:T(8,128)(2,1)S(1)}, u32[]{:S(2)}, u32[]{:S(2)}) collective-permute-start(bf16[512,128]{1,0:T(8,128)(2,1)S(1)} %pack.1.refs_0_), channel_id=1, source_target_pairs={{0,8},{8,0},{16,24},{24,16},{1,9},{9,1},{17,25},{25,17},{2,10},{10... | collective-permute-start | bytes 393224 | tf_op jit(solution)/shard_map/ppermute | solution.py:28
  9.2 2.0 %collective-permute-done.1.refs_1_ = bf16[32,1024]{1,0:T(8,128)(2,1)S(1)} collective-permute-done((bf16[32,1024]{1,0:T(8,128)(2,1)S(1)}, bf16[32,1024]{1,0:T(8,128)(2,1)S(1)}, u32[]{:S(2)}, u32[]{:S(2)}) %collective-permute-start.1) | collective-permute-done | bytes 65568 | tf_op jit(solution)/shard_map/ppermute | solution.py:28
  11.2 1.3 %collective-permute-start.2 = (bf16[512,128]{1,0:T(8,128)(2,1)S(1)}, bf16[512,128]{1,0:T(8,128)(2,1)S(1)}, u32[]{:S(2)}, u32[]{:S(2)}) collective-permute-start(bf16[512,128]{1,0:T(8,128)(2,1)S(1)} %after.3), channel_id=1, source_target_pairs={{0,16},{8,24},{16,0},{24,8},{1,17},{9,25},{17,1},{25,9},{2,18},{10... | collective-permute-start | bytes 393224 | tf_op jit(solution)/shard_map/ppermute | solution.py:28
  12.5 0.8 %collective-permute-done.3.refs_2_ = bf16[32,1024]{1,0:T(8,128)(2,1)S(1)} collective-permute-done((bf16[32,1024]{1,0:T(8,128)(2,1)S(1)}, bf16[32,1024]{1,0:T(8,128)(2,1)S(1)}, u32[]{:S(2)}, u32[]{:S(2)}) %collective-permute-start.3) | collective-permute-done | bytes 65568 | tf_op jit(solution)/shard_map/ppermute | solution.py:28
  13.2 2.5 %collective-permute-start.11 = (bf16[96,1024]{1,0:T(8,128)(2,1)S(1)}, bf16[96,1024]{1,0:T(8,128)(2,1)S(1)}, u32[]{:S(2)}, u32[]{:S(2)}) collective-permute-start(bf16[96,1024]{1,0:T(8,128)(2,1)S(1)} %join.1.refs_1_.refs_0_), channel_id=1, source_target_pairs={{0,6},{2,4},{4,2},{6,0},{1,7},{3,5},{5,3},{7,1},{8,14},{10,12},{12... | collective-permute-start | bytes 589832 | tf_op jit(solution)/shard_map/ppermute | solution.py:28
  15.8 0.5 %collective-permute-start.10 = (bf16[96,1024]{1,0:T(8,128)(2,1)S(1)}, bf16[96,1024]{1,0:T(8,128)(2,1)S(1)}, u32[]{:S(2)}, u32[]{:S(2)}) collective-permute-start(bf16[96,1024]{1,0:T(8,128)(2,1)S(1)} %join.1.refs_1_.refs_0_), channel_id=1, source_target_pairs={{0,4},{2,6},{4,0},{6,2},{1,5},{3,7},{5,1},{7,3},{8,12},{10,14},{12... | collective-permute-start | bytes 589832 | tf_op jit(solution)/shard_map/ppermute | solution.py:28
  16.3 0.5 %collective-permute-start.9 = (bf16[96,1024]{1,0:T(8,128)(2,1)S(1)}, bf16[96,1024]{1,0:T(8,128)(2,1)S(1)}, u32[]{:S(2)}, u32[]{:S(2)}) collective-permute-start(bf16[96,1024]{1,0:T(8,128)(2,1)S(1)} %join.1.refs_1_.refs_0_), channel_id=1, source_target_pairs={{0,2},{2,0},{4,6},{6,4},{1,3},{3,1},{5,7},{7,5},{8,10},{10,8},{12,... | collective-permute-start | bytes 589832 | tf_op jit(solution)/shard_map/ppermute | solution.py:28
  16.8 1.9 %collective-permute-done.2.refs_0_ = bf16[512,128]{1,0:T(8,128)(2,1)S(1)} collective-permute-done((bf16[512,128]{1,0:T(8,128)(2,1)S(1)}, bf16[512,128]{1,0:T(8,128)(2,1)S(1)}, u32[]{:S(2)}, u32[]{:S(2)}) %collective-permute-start.2) | collective-permute-done | bytes 131104 | tf_op jit(solution)/shard_map/ppermute | solution.py:28
  18.7 0.0 collective-permute-done.4.refs_2_.refs_0_
  18.7 0.1 collective-permute-start.7
  18.8 0.1 collective-permute-start.6
  18.9 3.9 %own_term.1 = (f32[4,512,1024]{2,1,0:T(8,128)S(1)}, bf16[3,512,1024]{2,1,0:T(8,128)(2,1)S(1)}, bf16[128,512]{1,0:T(8,128)(2,1)S(1)}, bf16[128,1024]{1,0:T(8,128)(2,1)S(1)}) custom-call(s32[4,4]{1,0:T(4,128)} %q_ref.1, bf16[4,512,1024]{2,1,0:T(8,128)(2,1)} %w_ref.1, bf16[512,128]{1,0:T(8,128)(2,1)} %bitcast.8, bf16[128,512]{1,0:T(8,128)(2,1)} %bitcast.10, ...), custom_call_target="tpu_custom_call" | custom-call | bytes 8388608 | tf_op jit(solution)/shard_map/own_term/pallas_call | solution.py:294
  22.8 0.0 collective-permute-done.11.refs_3_
  22.8 0.5 %collective-permute-start.5 = (bf16[512,128]{1,0:T(8,128)(2,1)S(1)}, bf16[512,128]{1,0:T(8,128)(2,1)S(1)}, u32[]{:S(2)}, u32[]{:S(2)}) collective-permute-start(bf16[512,128]{1,0:T(8,128)(2,1)S(1)} %collective-permute-done.4.refs_2_.refs_0_), channel_id=1, source_target_pairs={{0,1},{1,0},{2,3},{3,2},{4,5},{5,4},{6,7},{7,6},{8,9},{9,8},{10,11... | collective-permute-start | bytes 393224 | tf_op jit(solution)/shard_map/ppermute | solution.py:28
  23.4 0.4 collective-permute-done.7.refs_5_
  23.7 0.0 collective-permute-start.8
  23.7 0.0 collective-permute-done.10.refs_2_
  23.7 0.0 collective-permute-done.9.refs_1_
  23.7 0.1 spread.1.refs_7_
  23.8 0.0 collective-permute-done.6.refs_3_
  23.8 0.5 %collective-permute-done.5.refs_1_ = bf16[512,128]{1,0:T(8,128)(2,1)S(1)} collective-permute-done((bf16[512,128]{1,0:T(8,128)(2,1)S(1)}, bf16[512,128]{1,0:T(8,128)(2,1)S(1)}, u32[]{:S(2)}, u32[]{:S(2)}) %collective-permute-start.5) | collective-permute-done | bytes 131104 | tf_op jit(solution)/shard_map/ppermute | solution.py:28
  24.4 0.5 %panels.1.refs_4_ = bf16[2,4,512,128]{3,2,1,0:T(8,128)(2,1)S(1)} custom-call(bf16[512,128]{1,0:T(8,128)(2,1)S(1)} %collective-permute-done.4.refs_2_.refs_0_, bf16[512,128]{1,0:T(8,128)(2,1)S(1)} %collective-permute-done.5.refs_1_, bf16[512,128]{1,0:T(8,128)(2,1)S(1)} %after.4.after_ref.refs_2_, bf16[512,128]{1,0:T(8,128)(2,1)S(1)} %collective-permute-done.6.refs_3_), custom_call_target="tpu_custom_call" | custom-call | flops 1000000000 | tf_op jit(solution)/shard_map/panels/pallas_call | solution.py:321
  24.9 0.2 collective-permute-done.8.refs_6_
  25.1 5.2 %direct_term.1 = (f32[4,64,128]{2,1,0:T(8,128)S(1)}, bf16[4,64,128]{2,1,0:T(8,128)(2,1)S(1)}) custom-call(f32[4,512,1024]{2,1,0:T(8,128)S(1)} %get-tuple-element.11.refs_0_, bf16[3,512,1024]{2,1,0:T(8,128)(2,1)S(1)} %get-tuple-element.12.refs_1_, bf16[128,512]{1,0:T(8,128)(2,1)S(1)} %get-tuple-element.13.refs_2_, ...), custom_call_target="tpu_custom_call" | custom-call | tf_op jit(solution)/shard_map/direct_term/pallas_call | solution.py:349
  30.3 0.2 collective-permute-start.12
  30.6 1.1 %collective-permute-done.12 = bf16[4,64,128]{2,1,0:T(8,128)(2,1)S(1)} collective-permute-done((bf16[4,64,128]{2,1,0:T(8,128)(2,1)S(1)}, bf16[4,64,128]{2,1,0:T(8,128)(2,1)S(1)}, u32[]{:S(2)}, u32[]{:S(2)}) %collective-permute-start.12) | collective-permute-done | bytes 65568 | tf_op jit(solution)/shard_map/ppermute | solution.py:28
  31.7 2.5 %collective-permute-start.13 = (bf16[4,64,128]{2,1,0:T(8,128)(2,1)S(1)}, bf16[4,64,128]{2,1,0:T(8,128)(2,1)S(1)}, u32[]{:S(2)}, u32[]{:S(2)}) collective-permute-start(bf16[4,64,128]{2,1,0:T(8,128)(2,1)S(1)} %add_convert_fusion), channel_id=1, source_target_pairs={{0,6},{2,4},{4,2},{6,0},{1,7},{3,5},{5,3},{7,1},{8,14},{10,12},{12... | collective-permute-start | bytes 196616 | tf_op jit(solution)/shard_map/ppermute | solution.py:28
  34.2 0.5 %collective-permute-start.15 = (bf16[4,64,128]{2,1,0:T(8,128)(2,1)S(1)}, bf16[4,64,128]{2,1,0:T(8,128)(2,1)S(1)}, u32[]{:S(2)}, u32[]{:S(2)}) collective-permute-start(bf16[4,64,128]{2,1,0:T(8,128)(2,1)S(1)} %add_convert_fusion), channel_id=1, source_target_pairs={{0,2},{2,0},{4,6},{6,4},{1,3},{3,1},{5,7},{7,5},{8,10},{10,8},{12,... | collective-permute-start | bytes 196616 | tf_op jit(solution)/shard_map/ppermute | solution.py:28
  34.7 0.5 %collective-permute-start.14 = (bf16[4,64,128]{2,1,0:T(8,128)(2,1)S(1)}, bf16[4,64,128]{2,1,0:T(8,128)(2,1)S(1)}, u32[]{:S(2)}, u32[]{:S(2)}) collective-permute-start(bf16[4,64,128]{2,1,0:T(8,128)(2,1)S(1)} %add_convert_fusion), channel_id=1, source_target_pairs={{0,4},{2,6},{4,0},{6,2},{1,5},{3,7},{5,1},{7,3},{8,12},{10,14},{12... | collective-permute-start | bytes 196616 | tf_op jit(solution)/shard_map/ppermute | solution.py:28
  35.2 2.0 %collective-permute-done.13.refs_0_ = bf16[4,64,128]{2,1,0:T(8,128)(2,1)S(1)} collective-permute-done((bf16[4,64,128]{2,1,0:T(8,128)(2,1)S(1)}, bf16[4,64,128]{2,1,0:T(8,128)(2,1)S(1)}, u32[]{:S(2)}, u32[]{:S(2)}) %collective-permute-start.13) | collective-permute-done | bytes 65568 | tf_op jit(solution)/shard_map/ppermute | solution.py:28
  37.3 1.2 %collective-permute-done.15 = bf16[4,64,128]{2,1,0:T(8,128)(2,1)S(1)} collective-permute-done((bf16[4,64,128]{2,1,0:T(8,128)(2,1)S(1)}, bf16[4,64,128]{2,1,0:T(8,128)(2,1)S(1)}, u32[]{:S(2)}, u32[]{:S(2)}) %collective-permute-start.15) | collective-permute-done | bytes 65568 | tf_op jit(solution)/shard_map/ppermute | solution.py:28
  38.5 0.5 %collective-permute-done.14 = bf16[4,64,128]{2,1,0:T(8,128)(2,1)S(1)} collective-permute-done((bf16[4,64,128]{2,1,0:T(8,128)(2,1)S(1)}, bf16[4,64,128]{2,1,0:T(8,128)(2,1)S(1)}, u32[]{:S(2)}, u32[]{:S(2)}) %collective-permute-start.14) | collective-permute-done | bytes 65568 | tf_op jit(solution)/shard_map/ppermute | solution.py:28
  39.0 0.7 %add_bitcast_fusion = f32[1,4,64,128]{3,2,1,0:T(8,128)} fusion(bf16[4,64,128]{2,1,0:T(8,128)(2,1)S(1)} %add_convert_fusion, bf16[4,64,128]{2,1,0:T(8,128)(2,1)S(1)} %collective-permute-done.15, bf16[4,64,128]{2,1,0:T(8,128)(2,1)S(1)} %collective-permute-done.14, bf16[4,64,128]{2,1,0:T(8,128)(2,1)S(1)} %after.5), kind=kLoop, calls=%fused_computation | loop fusion | flops 229376 | bytes 393216 | tf_op jit(solution)/shard_map/broadcast_in_dim | solution.py:377
  (5 shorter events, 0.1 us)
Async XLA Ops:
  0.8 5.6 %collective-permute-start = (bf16[32,1024]{1,0:T(8,128)(2,1)S(1)}, bf16[32,1024]{1,0:T(8,128)(2,1)S(1)}, u32[]{:S(2)}, u32[]{:S(2)}) collective-permute-start(bf16[32,1024]{1,0:T(8,128)(2,1)S(1)} %dynamic-slice_bitcast_fusion), channel_id=1, source_target_pairs={{0,8},{8,0},{16,24},{24,16},{1,9},{9,1},{17,25},{25,17},{2,10},{10... | collective-permute-start | bytes 196616 | tf_op jit(solution)/shard_map/ppermute | solution.py:28
  3.9 7.3 %collective-permute-start.1 = (bf16[32,1024]{1,0:T(8,128)(2,1)S(1)}, bf16[32,1024]{1,0:T(8,128)(2,1)S(1)}, u32[]{:S(2)}, u32[]{:S(2)}) collective-permute-start(bf16[32,1024]{1,0:T(8,128)(2,1)S(1)} %dynamic-slice_bitcast_fusion), channel_id=1, source_target_pairs={{0,16},{8,24},{16,0},{24,8},{1,17},{9,25},{17,1},{25,9},{2,18},{10... | collective-permute-start | bytes 196616 | tf_op jit(solution)/shard_map/ppermute | solution.py:28
  6.5 6.8 %collective-permute-start.3 = (bf16[32,1024]{1,0:T(8,128)(2,1)S(1)}, bf16[32,1024]{1,0:T(8,128)(2,1)S(1)}, u32[]{:S(2)}, u32[]{:S(2)}) collective-permute-start(bf16[32,1024]{1,0:T(8,128)(2,1)S(1)} %dynamic-slice_bitcast_fusion), channel_id=1, source_target_pairs={{0,24},{8,16},{16,8},{24,0},{1,25},{9,17},{17,9},{25,1},{2,26},{10... | collective-permute-start | bytes 196616 | tf_op jit(solution)/shard_map/ppermute | solution.py:28
  7.4 11.3 %collective-permute-start.4 = (bf16[512,128]{1,0:T(8,128)(2,1)S(1)}, bf16[512,128]{1,0:T(8,128)(2,1)S(1)}, u32[]{:S(2)}, u32[]{:S(2)}) collective-permute-start(bf16[512,128]{1,0:T(8,128)(2,1)S(1)} %pack.1.refs_0_), channel_id=1, source_target_pairs={{0,8},{8,0},{16,24},{24,16},{1,9},{9,1},{17,25},{25,17},{2,10},{10... | collective-permute-start | bytes 393224 | tf_op jit(solution)/shard_map/ppermute | solution.py:28
  11.2 7.5 %collective-permute-start.2 = (bf16[512,128]{1,0:T(8,128)(2,1)S(1)}, bf16[512,128]{1,0:T(8,128)(2,1)S(1)}, u32[]{:S(2)}, u32[]{:S(2)}) collective-permute-start(bf16[512,128]{1,0:T(8,128)(2,1)S(1)} %after.3), channel_id=1, source_target_pairs={{0,16},{8,24},{16,0},{24,8},{1,17},{9,25},{17,1},{25,9},{2,18},{10... | collective-permute-start | bytes 393224 | tf_op jit(solution)/shard_map/ppermute | solution.py:28
  13.2 9.6 %collective-permute-start.11 = (bf16[96,1024]{1,0:T(8,128)(2,1)S(1)}, bf16[96,1024]{1,0:T(8,128)(2,1)S(1)}, u32[]{:S(2)}, u32[]{:S(2)}) collective-permute-start(bf16[96,1024]{1,0:T(8,128)(2,1)S(1)} %join.1.refs_1_.refs_0_), channel_id=1, source_target_pairs={{0,6},{2,4},{4,2},{6,0},{1,7},{3,5},{5,3},{7,1},{8,14},{10,12},{12... | collective-permute-start | bytes 589832 | tf_op jit(solution)/shard_map/ppermute | solution.py:28
  15.8 8.0 %collective-permute-start.10 = (bf16[96,1024]{1,0:T(8,128)(2,1)S(1)}, bf16[96,1024]{1,0:T(8,128)(2,1)S(1)}, u32[]{:S(2)}, u32[]{:S(2)}) collective-permute-start(bf16[96,1024]{1,0:T(8,128)(2,1)S(1)} %join.1.refs_1_.refs_0_), channel_id=1, source_target_pairs={{0,4},{2,6},{4,0},{6,2},{1,5},{3,7},{5,1},{7,3},{8,12},{10,14},{12... | collective-permute-start | bytes 589832 | tf_op jit(solution)/shard_map/ppermute | solution.py:28
  16.3 7.5 %collective-permute-start.9 = (bf16[96,1024]{1,0:T(8,128)(2,1)S(1)}, bf16[96,1024]{1,0:T(8,128)(2,1)S(1)}, u32[]{:S(2)}, u32[]{:S(2)}) collective-permute-start(bf16[96,1024]{1,0:T(8,128)(2,1)S(1)} %join.1.refs_1_.refs_0_), channel_id=1, source_target_pairs={{0,2},{2,0},{4,6},{6,4},{1,3},{3,1},{5,7},{7,5},{8,10},{10,8},{12,... | collective-permute-start | bytes 589832 | tf_op jit(solution)/shard_map/ppermute | solution.py:28
  18.7 5.0 %collective-permute-start.7 = (bf16[512,128]{1,0:T(8,128)(2,1)S(1)}, bf16[512,128]{1,0:T(8,128)(2,1)S(1)}, u32[]{:S(2)}, u32[]{:S(2)}) collective-permute-start(bf16[512,128]{1,0:T(8,128)(2,1)S(1)} %after.4.after_ref.refs_2_), channel_id=1, source_target_pairs={{0,8},{8,0},{16,24},{24,16},{1,9},{9,1},{17,25},{25,17},{2,10},{10... | collective-permute-start | bytes 393224 | tf_op jit(solution)/shard_map/ppermute | solution.py:28
  18.8 5.0 %collective-permute-start.6 = (bf16[512,128]{1,0:T(8,128)(2,1)S(1)}, bf16[512,128]{1,0:T(8,128)(2,1)S(1)}, u32[]{:S(2)}, u32[]{:S(2)}) collective-permute-start(bf16[512,128]{1,0:T(8,128)(2,1)S(1)} %after.4.after_ref.refs_2_), channel_id=1, source_target_pairs={{0,1},{1,0},{2,3},{3,2},{4,5},{5,4},{6,7},{7,6},{8,9},{9,8},{10,11... | collective-permute-start | bytes 393224 | tf_op jit(solution)/shard_map/ppermute | solution.py:28
  22.8 1.5 %collective-permute-start.5 = (bf16[512,128]{1,0:T(8,128)(2,1)S(1)}, bf16[512,128]{1,0:T(8,128)(2,1)S(1)}, u32[]{:S(2)}, u32[]{:S(2)}) collective-permute-start(bf16[512,128]{1,0:T(8,128)(2,1)S(1)} %collective-permute-done.4.refs_2_.refs_0_), channel_id=1, source_target_pairs={{0,1},{1,0},{2,3},{3,2},{4,5},{5,4},{6,7},{7,6},{8,9},{9,8},{10,11... | collective-permute-start | bytes 393224 | tf_op jit(solution)/shard_map/ppermute | solution.py:28
  23.7 1.3 %collective-permute-start.8 = (bf16[512,128]{1,0:T(8,128)(2,1)S(1)}, bf16[512,128]{1,0:T(8,128)(2,1)S(1)}, u32[]{:S(2)}, u32[]{:S(2)}) collective-permute-start(bf16[512,128]{1,0:T(8,128)(2,1)S(1)} %collective-permute-done.7.refs_5_), channel_id=1, source_target_pairs={{0,1},{1,0},{2,3},{3,2},{4,5},{5,4},{6,7},{7,6},{8,9},{9,8},{10,11... | collective-permute-start | bytes 393224 | tf_op jit(solution)/shard_map/ppermute | solution.py:28
  30.3 1.3 %collective-permute-start.12 = (bf16[4,64,128]{2,1,0:T(8,128)(2,1)S(1)}, bf16[4,64,128]{2,1,0:T(8,128)(2,1)S(1)}, u32[]{:S(2)}, u32[]{:S(2)}) collective-permute-start(bf16[4,64,128]{2,1,0:T(8,128)(2,1)S(1)} %get-tuple-element.16), channel_id=1, source_target_pairs={{0,1},{1,0},{2,3},{3,2},{4,5},{5,4},{6,7},{7,6},{8,9},{9,8},{10,11... | collective-permute-start | bytes 196616 | tf_op jit(solution)/shard_map/ppermute | solution.py:28
  31.7 5.6 %collective-permute-start.13 = (bf16[4,64,128]{2,1,0:T(8,128)(2,1)S(1)}, bf16[4,64,128]{2,1,0:T(8,128)(2,1)S(1)}, u32[]{:S(2)}, u32[]{:S(2)}) collective-permute-start(bf16[4,64,128]{2,1,0:T(8,128)(2,1)S(1)} %add_convert_fusion), channel_id=1, source_target_pairs={{0,6},{2,4},{4,2},{6,0},{1,7},{3,5},{5,3},{7,1},{8,14},{10,12},{12... | collective-permute-start | bytes 196616 | tf_op jit(solution)/shard_map/ppermute | solution.py:28
  34.2 4.3 %collective-permute-start.15 = (bf16[4,64,128]{2,1,0:T(8,128)(2,1)S(1)}, bf16[4,64,128]{2,1,0:T(8,128)(2,1)S(1)}, u32[]{:S(2)}, u32[]{:S(2)}) collective-permute-start(bf16[4,64,128]{2,1,0:T(8,128)(2,1)S(1)} %add_convert_fusion), channel_id=1, source_target_pairs={{0,2},{2,0},{4,6},{6,4},{1,3},{3,1},{5,7},{7,5},{8,10},{10,8},{12,... | collective-permute-start | bytes 196616 | tf_op jit(solution)/shard_map/ppermute | solution.py:28
  34.7 4.3 %collective-permute-start.14 = (bf16[4,64,128]{2,1,0:T(8,128)(2,1)S(1)}, bf16[4,64,128]{2,1,0:T(8,128)(2,1)S(1)}, u32[]{:S(2)}, u32[]{:S(2)}) collective-permute-start(bf16[4,64,128]{2,1,0:T(8,128)(2,1)S(1)} %add_convert_fusion), channel_id=1, source_target_pairs={{0,4},{2,6},{4,0},{6,2},{1,5},{3,7},{5,1},{7,3},{8,12},{10,14},{12... | collective-permute-start | bytes 196616 | tf_op jit(solution)/shard_map/ppermute | solution.py:28
